TPU v7x, 32 devices: a whole 2x2x4 slice. The times are simulated.
32 devices in a mesh: src: 2 (over y), dst: 16 (over z, x, core).
Axes of the slice: x: 2, y: 2, z: 4, core: 2. Of those that a mesh axis runs over, the one named last changes fastest.
Arguments:
- node_feats: bfloat16 [512, 256], P(('dst', 'src')), may hold values from -6 to 6
- cotangent: bfloat16 [512, 256], P(('src', 'dst')), may hold values from -6 to 6
- edge_attr: bfloat16 [49152, 128], P(('src', 'dst')), may hold values from -6 to 6
- src_ids: int32 [49152], P(('src', 'dst')), may hold values from 0 to 31
- dst_rel: int32 [49152], P(('src', 'dst')), may hold values from 0 to 127
- offsets: int32 [384], P(('src', 'dst')), may hold values from 0 to 128
- counts: int32 [384], P(('src', 'dst')), may hold values from 32 to 128
- w_node: bfloat16 [256, 512], replicated, may hold values from -0.375 to 0.375
- w_edge: bfloat16 [128, 512], replicated, may hold values from -0.5 to 0.5
- bias: float32 [512], replicated, may hold values from -3 to 3
- w_out: bfloat16 [512, 256], replicated, may hold values from -0.03125 to 0.03125
Outputs:
- aggregated: bfloat16 [512, 256], P(('src', 'dst'))
- node_grads: bfloat16 [512, 256], P(('dst', 'src'))
- attr_grads: bfloat16 [49152, 128], P(('src', 'dst'))
Inputs may be any that keep to these rules, and one draw needn't show every extreme that they name: `counts`: slots at or after a block's count carry no edge; their ids are arbitrary within range.
All inputs are finite; a program needn't handle non-finite values.
Results may differ from a plain program's by a relative error of at most 0.0049.
Values may be sent and summed in bfloat16 or wider, within the bound.
No kernel may reach another device: no remote copies, remote signals or barrier semaphores. Data moves between devices by JAX's collectives and lax.ppermute only.
A program may use at most 64 MiB of HBM per device.

v0:
```python
import jax
import jax.numpy as jnp
from jax import lax
from jax.sharding import PartitionSpec as P


def first_layer(x_edges, edge_attr, w_node, w_edge, bias):
    return (
        jnp.dot(x_edges, w_node, preferred_element_type=jnp.float32)
        + jnp.dot(edge_attr, w_edge, preferred_element_type=jnp.float32)
        + bias
    )


def local(
    node_feats, cotangent, edge_attr, src_ids, dst_rel, offsets, counts, w_node, w_edge, bias, w_out
):
    edges = src_ids.shape[0]
    blocks = offsets.shape[0]
    width = edges // blocks
    owned = node_feats.shape[0]
    feat = node_feats.shape[1]
    dst_rows = owned * lax.axis_size("dst")
    slots = lax.broadcasted_iota(jnp.int32, (blocks, width), 1)
    valid_grid = slots < counts[:, None]
    rel_grid = dst_rel.reshape(blocks, width)
    window_iota = lax.broadcasted_iota(jnp.int32, (blocks, width, width), 2)
    dst_hot = ((rel_grid[:, :, None] == window_iota) & valid_grid[:, :, None]).astype(jnp.float32)
    group = lax.all_gather(node_feats, "src", axis=0, tiled=True)
    group_rows = group.shape[0]
    src_hot = (src_ids[:, None] == lax.broadcasted_iota(jnp.int32, (edges, group_rows), 1)).astype(
        jnp.bfloat16
    )
    x_edges = jnp.dot(src_hot, group, preferred_element_type=jnp.float32).astype(jnp.bfloat16)
    pre = first_layer(x_edges, edge_attr, w_node, w_edge, bias)
    hidden = jax.nn.silu(pre).astype(jnp.bfloat16)
    message = jnp.dot(hidden, w_out, preferred_element_type=jnp.float32)
    block_sums = jnp.einsum(
        "bjr,bjw->brw",
        dst_hot,
        message.reshape(blocks, width, feat),
        precision=lax.Precision.HIGHEST,
    )

    def add_block(index, total):
        start = offsets[index]
        current = lax.dynamic_slice_in_dim(total, start, width, 0)
        return lax.dynamic_update_slice_in_dim(total, current + block_sums[index], start, 0)

    partial_sums = lax.fori_loop(0, blocks, add_block, jnp.zeros((dst_rows, feat), jnp.float32))
    aggregated = lax.psum_scatter(partial_sums, "dst", scatter_dimension=0, tiled=True)
    gathered = lax.all_gather(cotangent, "dst", axis=0, tiled=True)
    windows = jax.vmap(lambda start: lax.dynamic_slice_in_dim(gathered, start, width, 0))(offsets)
    d_message = (
        jnp.einsum(
            "bjr,brw->bjw",
            dst_hot.astype(jnp.bfloat16),
            windows,
            preferred_element_type=jnp.float32,
        )
        .astype(jnp.bfloat16)
        .reshape(edges, feat)
    )
    d_hidden = jnp.dot(d_message, w_out.T, preferred_element_type=jnp.float32)
    sig = jax.nn.sigmoid(pre)
    d_pre = (d_hidden * sig * (1.0 + pre * (1.0 - sig))).astype(jnp.bfloat16)
    attr_grads = jnp.dot(d_pre, w_edge.T, preferred_element_type=jnp.float32).astype(jnp.bfloat16)
    d_source = jnp.dot(d_pre, w_node.T, preferred_element_type=jnp.float32)
    source_sums = jnp.dot(src_hot.astype(jnp.float32).T, d_source, precision=lax.Precision.HIGHEST)
    node_grads = lax.psum_scatter(source_sums, "src", scatter_dimension=0, tiled=True)
    return (aggregated.astype(jnp.bfloat16), node_grads.astype(jnp.bfloat16), attr_grads)


def solution(mesh):
    in_specs = (
        P(("dst", "src"), None),
        P(("src", "dst"), None),
        P(("src", "dst"), None),
        P(("src", "dst")),
        P(("src", "dst")),
        P(("src", "dst")),
        P(("src", "dst")),
        P(),
        P(),
        P(),
        P(),
    )
    out_specs = (P(("src", "dst"), None), P(("dst", "src"), None), P(("src", "dst"), None))
    return jax.shard_map(local, mesh=mesh, in_specs=in_specs, out_specs=out_specs, check_vma=False)
```

profile of v0, /device:TPU:0, one launch (start us, length us, event | category | flops | bytes accessed | tf_op | source)
XLA Modules:
  0.0 182.9 jit_solution(17161848592903463955)
XLA Ops:
  8.0 23.6 %all_gather.7 = bf16[256,256]{1,0:T(8,128)(2,1)S(1)} all-gather(bf16[16,256]{1,0:T(8,128)(2,1)} %param.14), channel_id=1, replica_groups=mesh['src'=2,'dst'=16] {'dst'}, dimensions={0}, use_global_device_ids=true | all-gather | bytes 139264 | tf_op jit(solution)/shard_map/all_gather | solution.py:52
  32.3 15.3 %while.15 = (s32[]{:T(128)}, bf16[256,256]{1,0:T(8,128)(2,1)S(1)}, s32[12,2]{0,1:T(2,128)S(1)}, bf16[12,128,256]{2,1,0:T(8,128)(2,1)S(1)}, s32[]{:T(128)}) while((s32[]{:T(128)}, bf16[256,256]{1,0:T(8,128)(2,1)S(1)}, s32[12,2]{0,1:T(2,128)S(1)}, bf16[12,128,256]{2,1,0:T(8,128)(2,1)S(1)}, s32[]{:T(128)}) %tuple.46), condition=%wide.while_cond, body=%wide.while_body.sunk | while | flops 2 | bytes 131169 | solution.py:53
  47.7 4.6 %all_gather.6 = bf16[32,256]{1,0:T(8,128)(2,1)S(1)} all-gather(bf16[16,256]{1,0:T(8,128)(2,1)} %param.13), channel_id=1, replica_groups=mesh['src'=2,'dst'=16] {'src'}, dimensions={0}, use_global_device_ids=true | all-gather | bytes 24576 | tf_op jit(solution)/shard_map/all_gather | solution.py:29
  52.2 2.3 %convolution_convert_fusion.2 = bf16[12,128,256]{2,1,0:T(8,128)(2,1)} fusion(bf16[12,128,256]{2,1,0:T(8,128)(2,1)S(1)} %get-tuple-element.90, s32[12,128]{1,0:T(8,128)} %bitcast.35, pred[12,128]{1,0:T(8,128)(4,1)S(1)} %iota_compare_fusion.5), kind=kOutput, calls=%fused_computation.13 | convolution fusion | flops 101842944 | bytes 1580544 | tf_op jit(solution)/shard_map/bjr,brw->bjw/dot_general | solution.py:55
  54.5 1.8 fusion.4
  56.4 1.5 fusion.1
  58.0 1.4 fusion.2
  60.0 1.7 fusion.5
  61.8 4.0 %fusion.3 = f32[1536,256]{1,0:T(8,128)} fusion(bf16[512,256]{1,0:T(8,128)(2,1)S(1)} %copy-done.11, f32[1536,512]{1,0:T(8,128)} %copy-done.2), kind=kOutput, calls=%fused_computation.12 | convolution fusion | flops 406585344 | bytes 4980736 | tf_op jit(solution)/shard_map/dot_general | solution.py:37
  65.9 4.0 %fusion.7 = f32[12,128,256]{2,1,0:T(8,128)} fusion(f32[12,128,256]{2,1,0:T(8,128)} %bitcast.33, s32[12,128]{1,0:T(8,128)S(1)} %bitcast.36, pred[12,128]{1,0:T(8,128)(4,1)S(1)} %copy-done.9), kind=kOutput, calls=%fused_computation.20 | convolution fusion | flops 604372992 | bytes 3153408 | tf_op jit(solution)/shard_map/bjr,bjw->brw/dot_general | solution.py:38
  69.9 51.3 %while.14 = (s32[]{:T(128)}, f32[256,256]{1,0:T(8,128)S(1)}, s32[12]{0:T(128)S(1)}, f32[12,128,256]{2,1,0:T(8,128)}, s32[]{:T(128)}, /*index=5*/s32[]{:T(128)}, s32[]{:T(128)}) while((s32[]{:T(128)}, f32[256,256]{1,0:T(8,128)S(1)}, s32[12]{0:T(128)S(1)}, f32[12,128,256]{2,1,0:T(8,128)}, s32[]{:T(128)}, /*index=5*/s32[]{:T(128)}, ...), condition=%wide.region_1.2_spmd, body=%wide.region_0.1_spmd.sunk | while | flops 32773 | bytes 655495 | solution.py:50
  72.4 0.9 bitcast_add_fusion.2
  73.3 0.9 dynamic_update_slice.8
  76.8 0.9 bitcast_add_fusion.2
  81.1 0.9 bitcast_add_fusion.2
  85.3 0.9 bitcast_add_fusion.2
  86.2 0.8 dynamic_update_slice.8
  89.6 0.9 bitcast_add_fusion.2
  93.8 0.9 bitcast_add_fusion.2
  98.1 0.9 bitcast_add_fusion.2
  102.2 0.9 bitcast_add_fusion.2
  103.1 0.9 dynamic_update_slice.8
  106.6 0.9 bitcast_add_fusion.2
  107.5 0.9 dynamic_update_slice.8
  111.0 0.9 bitcast_add_fusion.2
  115.1 0.9 bitcast_add_fusion.2
  116.0 0.9 dynamic_update_slice.8
  119.5 0.9 bitcast_add_fusion.2
  121.9 1.3 convolution_convert_fusion.1
  123.2 1.3 convert_element_type.36
  124.5 50.3 %reduce-scatter.3.cloned.1.call-done = f32[16,256]{1,0:T(8,128)} async-done(((f32[256,256]{1,0:T(8,128)}), f32[16,256]{1,0:T(8,128)}) %reduce-scatter.3.cloned.1.call-update) | async-done | bytes 16400 | tf_op jit(solution)/shard_map/reduce_scatter | solution.py:51
  174.8 1.3 convert_element_type.31
  (92 shorter events, 30.0 us)
Async XLA Ops:
  7.2 49.2 %copy-start = (bf16[1536,128]{1,0:T(8,128)(2,1)S(1)}, bf16[1536,128]{1,0:T(8,128)(2,1)}, u32[]{:S(2)}) copy-start(bf16[1536,128]{1,0:T(8,128)(2,1)} %param.15) | copy-start | bytes 1179652
  7.2 116.0 %reduce-scatter.5.cloned.1.call-start = ((), (), s32[]{:S(2)}) async-start(), calls=%async_computation.3 | async-start | bytes 49152 | tf_op jit(solution)/shard_map/reduce_scatter | solution.py:70
  8.0 44.2 %copy-start.8 = (pred[12,128]{1,0:T(8,128)(4,1)}, pred[12,128]{1,0:T(8,128)(4,1)S(1)}, u32[]{:S(2)}) copy-start(pred[12,128]{1,0:T(8,128)(4,1)S(1)} %iota_compare_fusion.5) | copy-start | bytes 4612
  56.3 1.6 copy-start.4
  56.4 1.6 copy-start.10
  57.9 2.1 %copy-start.2 = (f32[1536,512]{1,0:T(8,128)}, f32[1536,512]{1,0:T(8,128)S(1)}, u32[]{:S(2)}) copy-start(f32[1536,512]{1,0:T(8,128)S(1)} %fusion.1) | copy-start | bytes 9437188
  57.9 1.4 copy-start.3
  59.3 0.7 copy-start.6
  59.4 2.5 %copy-start.11 = (bf16[512,256]{1,0:T(8,128)(2,1)S(1)}, bf16[512,256]{1,0:T(8,128)(2,1)}, u32[]{:S(2)}) copy-start(bf16[512,256]{1,0:T(8,128)(2,1)} %param.23) | copy-start | bytes 786436
  61.8 4.1 %copy-start.7 = (s32[1536]{0:T(1024)S(1)}, s32[1536]{0:T(1024)}, u32[]{:S(2)}) copy-start(s32[1536]{0:T(1024)} %param.17) | copy-start | bytes 18436
  61.8 4.1 %copy-start.9 = (pred[12,128]{1,0:T(8,128)(4,1)S(1)}, pred[12,128]{1,0:T(8,128)(4,1)}, u32[]{:S(2)}) copy-start(pred[12,128]{1,0:T(8,128)(4,1)} %copy-done.8) | copy-start | bytes 4612
  61.8 113.0 %reduce-scatter.3.cloned.1.call-start = ((), (), s32[]{:S(2)}) async-start(), calls=%async_computation.2 | async-start | bytes 278528 | tf_op jit(solution)/shard_map/reduce_scatter | solution.py:51
  65.8 4.0 %copy-start.12 = (s32[12]{0:T(128)S(1)}, s32[12]{0:T(128)}, u32[]{:S(2)}) copy-start(s32[12]{0:T(128)} %param.18) | copy-start | bytes 148
  65.8 56.0 %copy-start.5 = (bf16[128,512]{1,0:T(8,128)(2,1)S(1)}, bf16[128,512]{1,0:T(8,128)(2,1)}, u32[]{:S(2)}) copy-start(bf16[128,512]{1,0:T(8,128)(2,1)} %param.21) | copy-start | bytes 393220
  121.1 0.7 copy-start.1
Sparse Core Ops, SparseCore 0:
  61.9 7.0 reduce-scatter.4
  122.0 52.7 reduce-scatter.2
where the time goes:
time: 184 us; the launch traced here: 183 us
  waiting for transfers between devices  50.3 us (27%)
  local copies, waits for them, and re-layouts  32.4 us (18%)
  blocking collectives  28.2 us (15%)
  loops' own time  23.9 us (13%)
  matrix products  18.6 us (10%)
  other arithmetic  15.3 us (8%)
  between operations  14.2 us (8%)
    reduce_scatter x1, waiting for transfers between devices, local(): lax.psum_scatter(partial_sums, 'dst', scatter_dimension=0, tiled=True)  50.3 us
    all_gather x1, blocking collectives, local(): gathered = lax.all_gather(cotangent, 'dst', axis=0, tiled=True)  23.6 us
    another operation x1, loops' own time, local(): lax.fori_loop(0, blocks, add_block, jnp.zeros((dst_rows, feat), jnp.float...  23.6 us
    gather x36, local copies, waits for them, and re-layouts  15.1 us
    add x12, other arithmetic, add_block(): current + block_sums[index]  11.2 us
    dynamic_update_slice x12, local copies, waits for them, and re-layouts, add_block(): lax.dynamic_update_slice_in_dim(total, current + block_sums[index], start...  9.4 us
    dynamic_slice x12, local copies, waits for them, and re-layouts, add_block(): start = offsets[index]  7.04 us
    all_gather x1, blocking collectives, local(): group = lax.all_gather(node_feats, 'src', axis=0, tiled=True)  4.58 us
  transfers between devices with their start and end apart: 2, of which 1 were waited for; matrix products, arithmetic and copies ran while one was open for 21% of the time, Pallas kernels for 0%

commit v1 on v0

v1 whole, which is shorter than its diff:
```python
import math

import jax
import jax.numpy as jnp
from jax import lax
from jax.experimental import pallas as pl
from jax.experimental.pallas import tpu as pltpu
from jax.sharding import PartitionSpec as P

F32 = jnp.float32
BF16 = jnp.bfloat16
NN = (((1,), (0,)), ((), ()))
NT = (((1,), (1,)), ((), ()))
TN = (((0,), (0,)), ((), ()))
SMEM = pl.BlockSpec(memory_space=pltpu.SMEM)
VMEM = pl.BlockSpec(memory_space=pltpu.VMEM)
ANY = pl.BlockSpec(memory_space=pl.ANY)
CHUNK = 1536


def dot(a, b, dims=NN):
    return lax.dot_general(a, b, dims, preferred_element_type=F32)


def halves(x):
    high = x.astype(BF16)
    return high, (x - high.astype(F32)).astype(BF16)


def chunks(edges):
    return [pl.ds(c, min(CHUNK, edges - c)) for c in range(0, edges, CHUNK)]


def load(pairs, sems):
    copies = [pltpu.make_async_copy(*pair, sems.at[i]) for i, pair in enumerate(pairs)]
    for copy in copies:
        copy.start()
    return copies


def wait(copies):
    for copy in copies:
        copy.wait()


def edge_hots(off, cnt, rel, sid, dst_rows, src_rows):
    blocks, width = rel.shape
    lane = lax.broadcasted_iota(jnp.int32, (1, width), 1)
    dst_row = lax.broadcasted_iota(jnp.int32, (dst_rows, width), 0)
    src_row = lax.broadcasted_iota(jnp.int32, (src_rows, width), 0)
    for b in range(blocks):
        target = jnp.where(lane < cnt[b], rel[b : b + 1, :] + off[b], -1)
        to_dst = (dst_row == target).astype(F32)
        to_src = (src_row == sid[b : b + 1, :]).astype(F32)
        yield pl.ds(b * width, width), to_dst, to_src


def partner(me, n, k, back=False):
    if n & (n - 1) == 0:
        return me ^ k
    return lax.rem(me + (n - k if back else k), n)


def partner_of(me, n, k):
    return me ^ k if n & (n - 1) == 0 else (me + k) % n


def part(index, rows):
    return pl.ds(pl.multiple_of(index * rows, rows), rows)


INNER, NEAR = 4, 2
STEPS = (0, 2, 3, 1)


def place(index):
    return index // (NEAR * INNER), index // INNER % NEAR, index % INNER


def here():
    me = lax.axis_index("dst")
    return lax.div(me, NEAR * INNER), lax.rem(lax.div(me, INNER), NEAR), lax.rem(me, INNER)


def layer_steps(n_far):
    return [0, 1, *range(n_far * NEAR - 1, 1, -1)]


def layer_partner(far, near, n_far, k):
    return partner(far, n_far, k // NEAR) * NEAR + partner(near, NEAR, k % NEAR)


def swap(sends, to):
    pairs = [[(i, to(i, k)) for i in range(lax.axis_size("dst"))] for k in range(len(sends) + 1)]
    return [lax.ppermute(x, "dst", pairs[k + 1]) for k, x in enumerate(sends)]


def prepare(
    off_in, cnt_in, rel_in, sid_in, attr_in, cot_in, feat_in, bias_in, w_node_in, w_edge_in, w_out_in,
    rows_out, dst_out, src_out, cot_out, feat_out, bias_out, w_node_out, w_edge_out,
    w_out_out, off, cnt, rel, sid, sems,
):
    width = attr_in.shape[1]
    copies = load(
        [(off_in, off), (cnt_in, cnt), (rel_in, rel), (sid_in, sid)]
        + [(attr_in, rows_out.at[:, :width]), (cot_in, cot_out)]
        + [(feat_in, feat_out), (bias_in, bias_out)]
        + [(w_edge_in, w_edge_out), (w_node_in, w_node_out), (w_out_in, w_out_out)],
        sems,
    )
    wait(copies[:4])
    spare = rows_out.shape[1] - width - 2 * src_out.shape[0]
    fill = [jnp.zeros((spare, rel.shape[1]), F32)] if spare else []
    for at, to_dst, to_src in edge_hots(off, cnt, rel, sid, dst_out.shape[0], src_out.shape[0]):
        dst_out[:, at] = to_dst.astype(BF16)
        src_out[:, at] = to_src.astype(BF16)
        rows_out[at, width:] = jnp.concatenate([to_src, to_src, *fill], axis=0).T.astype(BF16)
    wait(copies[4:])


def forward(n_src, rows, dst_hot, bias, w_node, w_edge, w_out, *refs):
    feats, (half_out, sums_out, group, first, hidden) = refs[:n_src], refs[n_src:]
    me, owned = lax.axis_index("src"), feats[0].shape[0]
    for k, ref in enumerate(feats):
        group[part(lax.rem(me + k, n_src), owned), :] = ref[...]
    high, low = halves(0.5 * (dot(group[...], w_node[...]) + bias[...]))
    width, sources = w_edge.shape[0], group.shape[0]
    first[:width, :] = 0.5 * w_edge[...]
    first[width : width + sources, :] = high
    first[width + sources : width + 2 * sources, :] = low
    if first.shape[0] > width + 2 * sources:
        first[width + 2 * sources :, :] = jnp.zeros_like(first[width + 2 * sources :, :])
    for c in chunks(rows.shape[0]):
        half = dot(rows[c, :], first[...])
        half_out[c, :] = half
        hidden[c, :] = (half * jnp.tanh(half) + half).astype(BF16)
    high, low = halves(dot(dst_hot[...], hidden[...]))
    sums_out[...] = dot(high, w_out[...]) + dot(low, w_out[...])


def pack(n_far, owned, sums, *refs):
    parts, (cots_out, keep, *sends) = refs[:n_far], refs[n_far:]
    far, near, me = here()
    for k, ref in enumerate(parts):
        cots_out[part(partner(far, n_far, k, True), owned), :] = ref[...]
    rows = keep.shape[0]
    for k, out in enumerate([keep, *sends]):
        to = partner(me, INNER, STEPS[k])
        for z in range(n_far * NEAR):
            block = sums[part(z * INNER + to, owned), :]
            out[z * owned : (z + 1) * owned, :] = block.astype(out.dtype)
        if k:
            out[rows:, :] = cots_out[...]


def spread(n_far, owned, _, cots, keep, *refs):
    parts, (cots_out, own, *sends, total) = refs[: INNER - 1], refs[INNER - 1 :]
    far, near, me = here()
    rows = keep.shape[0]
    for k, ref in enumerate([cots] + [ref.at[rows:, :] for ref in parts]):
        owner = partner(me, INNER, STEPS[k], True)
        for f in range(n_far):
            block = ref[f * owned : (f + 1) * owned, :]
            cots_out[part(f * INNER + owner, owned), :] = block
    total[...] = sum((ref[:rows, :].astype(F32) for ref in parts), keep[...])
    for k, out in enumerate([own, *sends]):
        layer = layer_partner(far, near, n_far, layer_steps(n_far)[k])
        out[:owned, :] = total[part(layer, owned), :].astype(out.dtype)
    sends[0][owned:, :] = cots_out[...]


def slopes(_, half, dst_hot, slope_out, turned_out):
    for c in chunks(half.shape[0]):
        turned_out[c, :] = dst_hot[:, c].astype(F32).T.astype(BF16)
        t = jnp.tanh(half[c, :])
        slope_out[c, :] = 0.5 + 0.5 * (t + half[c, :] * (1.0 - t * t))


def backward(
    n_src, slope, dst_hot, src_hot, w_node, w_out, cots_near, came,
    d_pre, keep_out, send_out, total, cots,
):
    _, near, _ = here()
    owned, run = keep_out.shape[0], INNER * keep_out.shape[0]
    for f in range(cots_near.shape[0] // run):
        at = f * run
        cots[part(f * NEAR + near, run), :] = cots_near[at : at + run, :]
        at += owned
        cots[part(f * NEAR + 1 - near, run), :] = came[at : at + run, :]
    for c in chunks(slope.shape[0]):
        d_message = dot(dst_hot[c, :], cots[...]).astype(BF16)
        d_pre[c, :] = (dot(d_message, w_out[...], NT) * slope[c, :]).astype(BF16)
    high, low = halves(dot(src_hot[...], d_pre[...]))
    total[...] = dot(high, w_node[...], NT) + dot(low, w_node[...], NT)
    me = lax.axis_index("src")
    keep_out[...] = total[part(me, owned), :]
    for k in range(1, n_src):
        send_out[k - 1] = total[part(lax.rem(me + k, n_src), owned), :].astype(BF16)


def attributes(d_pre, w_edge, attr_out):
    for c in chunks(d_pre.shape[0]):
        attr_out[c, :] = dot(d_pre[c, :], w_edge[...], NT).astype(BF16)


def finish(n_agg, *refs):
    agg_out, grads_out = refs[-2:]
    owned = agg_out.shape[0]
    agg_out[...] = sum(ref[:owned, :].astype(F32) for ref in refs[:n_agg]).astype(BF16)
    grads_out[...] = sum(ref[...].astype(F32) for ref in refs[n_agg:-2]).astype(BF16)


def ahead(x, axis, k):
    n = lax.axis_size(axis)
    return lax.ppermute(x, axis, [((i + k) % n, i) for i in range(n)])


def local(
    node_feats, cotangent, edge_attr, src_ids, dst_rel, offsets, counts, w_node, w_edge, bias, w_out
):
    edges, attr_width = edge_attr.shape
    blocks = offsets.shape[0]
    width = edges // blocks
    owned, feat = node_feats.shape
    hidden = w_node.shape[1]
    n_src, n_dst = lax.axis_size("src"), lax.axis_size("dst")
    dst_rows, src_rows = owned * n_dst, owned * n_src
    n_far = n_dst // (NEAR * INNER)
    layers = n_far * NEAR
    params = pltpu.CompilerParams(vmem_limit_bytes=32 * 2**20)

    def array(*shape, dtype=BF16):
        return jax.ShapeDtypeStruct(shape, dtype)

    def rows_of(blocks, dtype=BF16):
        return array(blocks * owned, feat, dtype=dtype)

    def in_hbm(x):
        return pltpu.with_memory_space_constraint(x, pltpu.HBM)

    def call(kernel, name, args, outs, scratch=(), specs=None):
        return pl.pallas_call(
            kernel,
            name=name,
            in_specs=specs or [VMEM] * len(args),
            out_specs=[VMEM] * len(outs),
            out_shape=outs,
            scratch_shapes=list(scratch),
            compiler_params=params,
        )(*args)

    ints = [offsets, counts, dst_rel.reshape(blocks, width), src_ids.reshape(blocks, width)]
    bias = bias.reshape(1, hidden)
    feats = [ahead(node_feats, "src", k) for k in range(1, n_src)]
    depth = attr_width + 2 * src_rows
    depth += -depth % 128

    rows, dst_hot, src_hot, cots, own, *params_near = call(
        prepare,
        "prepare",
        [in_hbm(x) for x in (*ints, edge_attr, cotangent, node_feats, bias, w_node, w_edge, w_out)],
        [
            array(edges, depth),
            array(dst_rows, edges),
            array(src_rows, edges),
            rows_of(1),
            rows_of(1),
            array(*bias.shape, dtype=F32),
        ]
        + [array(*x.shape) for x in (w_node, w_edge, w_out)],
        [pltpu.SMEM(x.shape, jnp.int32) for x in ints[:2]]
        + [pltpu.VMEM(x.shape, jnp.int32) for x in ints[2:]]
        + [pltpu.SemaphoreType.DMA((11,))],
        [ANY] * 11,
    )
    _, w_node, w_edge, w_out = params_near

    def to_far(i, k):
        return i + (partner_of(place(i)[0], n_far, k) - place(i)[0]) * NEAR * INNER

    parts = swap([cotangent] * (n_far - 1), to_far)

    half, sums = call(
        lambda *refs: forward(n_src, *refs),
        "forward",
        [rows, dst_hot, *params_near, own, *feats],
        [array(edges, hidden, dtype=F32), rows_of(n_dst, F32)],
        [
            pltpu.VMEM((src_rows, feat), BF16),
            pltpu.VMEM((depth, hidden), BF16),
            pltpu.VMEM((edges, hidden), BF16),
        ],
    )

    cots, keep, *sends = call(
        lambda *refs: pack(n_far, owned, *refs),
        "pack",
        [sums, cots, *parts],
        [rows_of(n_far), rows_of(layers, F32)] + [rows_of(layers + n_far)] * (INNER - 1),
    )
    parts = swap(sends, lambda i, k: i - i % INNER + partner_of(i % INNER, INNER, STEPS[k]))

    slope, turned = call(
        slopes,
        "slopes",
        [keep, half, dst_hot],
        [array(edges, hidden, dtype=F32), array(edges, dst_rows)],
    )

    beside = n_far * INNER
    cots, keep, *sends = call(
        lambda *refs: spread(n_far, owned, *refs),
        "spread",
        [slope, cots, keep, *parts],
        [rows_of(beside), rows_of(1, F32), rows_of(1 + beside)] + [rows_of(1, F32)] * (layers - 2),
        [pltpu.VMEM((layers * owned, feat), F32)],
        [ANY] + [VMEM] * (1 + INNER),
    )

    def to_layer(i, k):
        far, near, me = place(i)
        k = layer_steps(n_far)[k]
        to = partner_of(far, n_far, k // NEAR) * NEAR + partner_of(near, NEAR, k % NEAR)
        return to * INNER + me

    parts = swap(sends, to_layer)

    d_pre, keep_grads, send_grads = call(
        lambda *refs: backward(n_src, *refs),
        "backward",
        [slope, turned, src_hot, w_node, w_out, cots, parts[0]],
        [array(edges, hidden), rows_of(1, F32), array(n_src - 1, owned, feat)],
        [pltpu.VMEM((src_rows, feat), F32), pltpu.VMEM((dst_rows, feat), BF16)],
    )

    others = [ahead(send_grads[k - 1], "src", n_src - k) for k in range(1, n_src)]

    (attr_grads,) = call(
        attributes,
        "attributes",
        [d_pre, w_edge],
        [array(edges, attr_width)],
    )

    aggregated, node_grads = call(
        lambda *refs: finish(1 + len(parts), *refs),
        "finish",
        [keep, *parts, keep_grads, *others],
        [rows_of(1), rows_of(1)],
    )
    return aggregated, node_grads, attr_grads


def solution(mesh):
    in_specs = (
        P(("dst", "src"), None),
        P(("src", "dst"), None),
        P(("src", "dst"), None),
        P(("src", "dst")),
        P(("src", "dst")),
        P(("src", "dst")),
        P(("src", "dst")),
        P(),
        P(),
        P(),
        P(),
    )
    out_specs = (P(("src", "dst"), None), P(("dst", "src"), None), P(("src", "dst"), None))
    return jax.shard_map(local, mesh=mesh, in_specs=in_specs, out_specs=out_specs, check_vma=False)
```

time: 184 us -> 24.7 us (0.13)
  waiting for transfers between devices: 50.3 us -> 3.92 us
  local copies, waits for them, and re-layouts: 32.4 us -> 0 us
  blocking collectives: 28.2 us -> 0 us
  loops' own time: 23.9 us -> 0 us
  matrix products: 18.6 us -> 0 us
  other arithmetic: 15.3 us -> 0 us
  between operations: 14.2 us -> 0.7 us
  starting transfers between devices: 0.08 us -> 11.9 us
  Pallas kernels: 0 us -> 8.02 us
    reduce_scatter x2 -> x0, waiting for transfers between devices: 50.3 us -> none  [the longest x1 50.3 us: local(): lax.psum_scatter(partial_sums, 'dst', scatter_dimension=0, tiled=True)]
    all_gather x2 -> x0, blocking collectives: 28.2 us -> none  [the longest x1 23.6 us: local(): gathered = lax.all_gather(cotangent, 'dst', axis=0, tiled=True)]
    another operation x2 -> x0, loops' own time: 23.9 us -> none  [the longest x1 23.6 us: local(): lax.fori_loop(0, blocks, add_block, jnp.zeros((dst_rows, feat), jnp.float...]
    dot_general x9 -> x0, matrix products: 18.6 us -> none  [the longest x1 4 us: local(): message = jnp.dot(hidden, w_out, preferred_element_type=jnp.float32)]
    gather x36 -> x0, local copies, waits for them, and re-layouts: 15.1 us -> none
    ppermute x0 -> x9, starting transfers between devices: none -> 11.9 us  [the longest x7 8.35 us: swap(): return [lax.ppermute(x, 'dst', pairs[k + 1]) for k, x in enumerate(sends)]]
    add x12 -> x0, other arithmetic: 11.2 us -> none  [add_block(): current + block_sums[index]]
    dynamic_update_slice x12 -> x0, local copies, waits for them, and re-layouts: 9.4 us -> none  [add_block(): lax.dynamic_update_slice_in_dim(total, current + block_sums[index], start...]
  transfers between devices with their start and end apart: 2 -> 9, of which waited for: 1 -> 5; matrix products, arithmetic and copies ran while one was open for 21% -> 0% of each run, Pallas kernels for 0% -> 30%
where the time goes in v1:
time: 24.7 us; the launch traced here: 24.6 us
  starting transfers between devices  11.9 us (48%)
  Pallas kernels  8.02 us (32%)
  waiting for transfers between devices  3.92 us (16%)
  between operations  0.7 us (3%)
    ppermute x7, starting transfers between devices, swap(): return [lax.ppermute(x, 'dst', pairs[k + 1]) for k, x in enumerate(sends)]  8.35 us
    pallas_call x8, Pallas kernels, call(): pl.pallas_call(kernel, name=name, in_specs=specs or [VMEM] * len(args), o...  8.02 us
    ppermute x2, starting transfers between devices, ahead(): return lax.ppermute(x, axis, [((i + k) % n, i) for i in range(n)])  3.57 us
    ppermute x7, waiting for transfers between devices, swap(): return [lax.ppermute(x, 'dst', pairs[k + 1]) for k, x in enumerate(sends)]  2.44 us
    ppermute x2, waiting for transfers between devices, ahead(): return lax.ppermute(x, axis, [((i + k) % n, i) for i in range(n)])  1.48 us
  transfers between devices with their start and end apart: 9, of which 5 were waited for; matrix products, arithmetic and copies ran while one was open for 0% of the time, Pallas kernels for 30%

profile of v1, /device:TPU:0, one launch (start us, length us, event | category | flops | bytes accessed | tf_op | source)
XLA Modules:
  0.0 24.6 jit_solution(17437549466509886121)
XLA Ops:
  0.6 3.0 %collective-permute-start = (bf16[16,256]{1,0:T(8,128)(2,1)}, bf16[16,256]{1,0:T(8,128)(2,1)S(1)}, u32[]{:S(2)}, u32[]{:S(2)}) collective-permute-start(bf16[16,256]{1,0:T(8,128)(2,1)} %feat_in.1), channel_id=1, source_target_pairs={{16,0},{0,16},{17,1},{1,17},{18,2},{2,18},{19,3},{3,19},{20,4},{4,... | collective-permute-start | bytes 24584 | tf_op jit(solution)/shard_map/ppermute | solution.py:215
  3.7 2.6 %collective-permute-start.1 = (bf16[16,256]{1,0:T(8,128)(2,1)}, bf16[16,256]{1,0:T(8,128)(2,1)S(1)}, u32[]{:S(2)}, u32[]{:S(2)}) collective-permute-start(bf16[16,256]{1,0:T(8,128)(2,1)} %cot_in.1), channel_id=1, source_target_pairs={{0,8},{1,9},{2,10},{3,11},{4,12},{5,13},{6,14},{7,15},{8,0},{9,1},... | collective-permute-start | bytes 24584 | tf_op jit(solution)/shard_map/ppermute | solution.py:95
  6.3 1.4 %prepare.1 = (bf16[1536,256]{1,0:T(8,128)(2,1)S(1)}, bf16[256,1536]{1,0:T(8,128)(2,1)S(1)}, bf16[32,1536]{1,0:T(8,128)(2,1)S(1)}, bf16[16,256]{1,0:T(8,128)(2,1)...) custom-call(s32[12]{0:T(128)} %off_in.1, ...), custom_call_target="tpu_custom_call" | custom-call | tf_op jit(solution)/shard_map/prepare/pallas_call | solution.py:242
  7.7 0.0 collective-permute-done.refs_7_
  7.7 1.5 %forward.1 = (f32[1536,512]{1,0:T(8,128)S(1)}, f32[256,256]{1,0:T(8,128)S(1)}) custom-call(bf16[1536,256]{1,0:T(8,128)(2,1)S(1)} %get-tuple-element.31.refs_0_, bf16[256,1536]{1,0:T(8,128)(2,1)S(1)} %get-tuple-element.32.refs_1_.dst_hot, f32[1,512]{1,0:T(1,128)S(1)} %get-tuple-element.33.refs_2_, bf16[256,512]{1,0:T(8,128)(2,1)S(1)} %get-tuple-element.34.refs_3_, ...), custom_call_target="tpu_custom_call" | custom-call | tf_op jit(solution)/shard_map/forward/pallas_call | solution.py:242
  9.2 0.0 collective-permute-done.1.refs_2_
  9.3 1.6 %collective-permute-start.2 = (bf16[96,256]{1,0:T(8,128)(2,1)S(1)}, bf16[96,256]{1,0:T(8,128)(2,1)S(1)}, u32[]{:S(2)}, u32[]{:S(2)}) collective-permute-start(bf16[96,256]{1,0:T(8,128)(2,1)S(1)} %get-tuple-element.44), channel_id=1, source_target_pairs={{0,2},{1,3},{2,0},{3,1},{4,6},{5,7},{6,4},{7,5},{8,10},{9,11},{10,... | collective-permute-start | bytes 147464 | tf_op jit(solution)/shard_map/ppermute | solution.py:95
  10.8 0.0 collective-permute-start.3
  10.8 0.6 %collective-permute-start.4 = (bf16[96,256]{1,0:T(8,128)(2,1)S(1)}, bf16[96,256]{1,0:T(8,128)(2,1)S(1)}, u32[]{:S(2)}, u32[]{:S(2)}) collective-permute-start(bf16[96,256]{1,0:T(8,128)(2,1)S(1)} %get-tuple-element.46), channel_id=1, source_target_pairs={{0,1},{1,0},{2,3},{3,2},{4,5},{5,4},{6,7},{7,6},{8,9},{9,8},{10,11... | collective-permute-start | bytes 147464 | tf_op jit(solution)/shard_map/ppermute | solution.py:95
  11.5 1.8 %slopes.1 = (f32[1536,512]{1,0:T(8,128)S(1)}, bf16[1536,256]{1,0:T(8,128)(2,1)S(1)}) custom-call(f32[64,256]{1,0:T(8,128)S(1)} %get-tuple-element.40._.refs_2_, f32[1536,512]{1,0:T(8,128)S(1)} %get-tuple-element.41.half, bf16[256,1536]{1,0:T(8,128)(2,1)S(1)} %get-tuple-element.32.refs_1_.dst_hot), custom_call_target="tpu_custom_call" | custom-call | tf_op jit(solution)/shard_map/slopes/pallas_call | solution.py:242
  13.3 0.2 collective-permute-done.2.refs_3_
  13.4 1.1 %collective-permute-done.3.refs_4_ = bf16[96,256]{1,0:T(8,128)(2,1)S(1)} collective-permute-done((bf16[96,256]{1,0:T(8,128)(2,1)S(1)}, bf16[96,256]{1,0:T(8,128)(2,1)S(1)}, u32[]{:S(2)}, u32[]{:S(2)}) %collective-permute-start.3) | collective-permute-done | bytes 49184 | tf_op jit(solution)/shard_map/ppermute | solution.py:95
  14.5 0.0 collective-permute-done.4.refs_5_
  14.5 1.6 %collective-permute-start.5 = (bf16[144,256]{1,0:T(8,128)(2,1)S(1)}, bf16[144,256]{1,0:T(8,128)(2,1)S(1)}, u32[]{:S(2)}, u32[]{:S(2)}) collective-permute-start(bf16[144,256]{1,0:T(8,128)(2,1)S(1)} %get-tuple-element.48), channel_id=1, source_target_pairs={{0,4},{1,5},{2,6},{3,7},{4,0},{5,1},{6,2},{7,3},{8,12},{9,13},{10,... | collective-permute-start | bytes 221192 | tf_op jit(solution)/shard_map/ppermute | solution.py:95
  16.2 1.7 %collective-permute-start.6 = (f32[16,256]{1,0:T(8,128)S(1)}, f32[16,256]{1,0:T(8,128)S(1)}, u32[]{:S(2)}, u32[]{:S(2)}) collective-permute-start(f32[16,256]{1,0:T(8,128)S(1)} %get-tuple-element.49), channel_id=1, source_target_pairs={{0,12},{1,13},{2,14},{3,15},{4,8},{5,9},{6,10},{7,11},{8,4},{9,5},... | collective-permute-start | bytes 49160 | tf_op jit(solution)/shard_map/ppermute | solution.py:95
  17.8 0.3 %collective-permute-start.7 = (f32[16,256]{1,0:T(8,128)S(1)}, f32[16,256]{1,0:T(8,128)S(1)}, u32[]{:S(2)}, u32[]{:S(2)}) collective-permute-start(f32[16,256]{1,0:T(8,128)S(1)} %get-tuple-element.50), channel_id=1, source_target_pairs={{0,8},{1,9},{2,10},{3,11},{4,12},{5,13},{6,14},{7,15},{8,0},{9,1},... | collective-permute-start | bytes 49160 | tf_op jit(solution)/shard_map/ppermute | solution.py:95
  18.1 0.9 %collective-permute-done.5.refs_6_.refs_1_ = bf16[144,256]{1,0:T(8,128)(2,1)S(1)} collective-permute-done((bf16[144,256]{1,0:T(8,128)(2,1)S(1)}, bf16[144,256]{1,0:T(8,128)(2,1)S(1)}, u32[]{:S(2)}, u32[]{:S(2)}) %collective-permute-start.5) | collective-permute-done | bytes 73760 | tf_op jit(solution)/shard_map/ppermute | solution.py:95
  18.9 1.3 %backward.1 = (bf16[1536,512]{1,0:T(8,128)(2,1)S(1)}, f32[16,256]{1,0:T(8,128)S(1)}, bf16[1,16,256]{2,1,0:T(8,128)(2,1)S(1)}) custom-call(f32[1536,512]{1,0:T(8,128)S(1)} %get-tuple-element.42.refs_0_, bf16[1536,256]{1,0:T(8,128)(2,1)S(1)} %get-tuple-element.51.refs_1_, bf16[32,1536]{1,0:T(8,128)(2,1)S(1)} %get-tuple-element.52.refs_2_, ...), custom_call_target="tpu_custom_call" | custom-call | tf_op jit(solution)/shard_map/backward/pallas_call | solution.py:242
  20.3 0.5 %collective-permute-start.8 = (bf16[16,256]{1,0:T(8,128)(2,1)S(1)}, bf16[16,256]{1,0:T(8,128)(2,1)S(1)}, u32[]{:S(2)}, u32[]{:S(2)}) collective-permute-start(bf16[16,256]{1,0:T(8,128)(2,1)S(1)} %bitcast.4), channel_id=1, source_target_pairs={{16,0},{0,16},{17,1},{1,17},{18,2},{2,18},{19,3},{3,19},{20,4},{4,... | collective-permute-start | bytes 24584 | tf_op jit(solution)/shard_map/ppermute | solution.py:215
  20.8 1.3 %attributes.1 = bf16[1536,128]{1,0:T(8,128)(2,1)} custom-call(bf16[1536,512]{1,0:T(8,128)(2,1)S(1)} %get-tuple-element.58.d_pre, bf16[128,512]{1,0:T(8,128)(2,1)S(1)} %get-tuple-element.35.refs_4_.w_edge), custom_call_target="tpu_custom_call" | custom-call | tf_op jit(solution)/shard_map/attributes/pallas_call | solution.py:242
  22.1 0.0 collective-permute-done.6.refs_2_
  22.1 0.3 %collective-permute-done.7.refs_3_ = f32[16,256]{1,0:T(8,128)S(1)} collective-permute-done((f32[16,256]{1,0:T(8,128)S(1)}, f32[16,256]{1,0:T(8,128)S(1)}, u32[]{:S(2)}, u32[]{:S(2)}) %collective-permute-start.7) | collective-permute-done | bytes 16416 | tf_op jit(solution)/shard_map/ppermute | solution.py:95
  22.5 1.5 %collective-permute-done.8.refs_5_ = bf16[16,256]{1,0:T(8,128)(2,1)S(1)} collective-permute-done((bf16[16,256]{1,0:T(8,128)(2,1)S(1)}, bf16[16,256]{1,0:T(8,128)(2,1)S(1)}, u32[]{:S(2)}, u32[]{:S(2)}) %collective-permute-start.8) | collective-permute-done | bytes 8224 | tf_op jit(solution)/shard_map/ppermute | solution.py:215
  23.9 0.6 %finish.1 = (bf16[16,256]{1,0:T(8,128)(2,1)}, bf16[16,256]{1,0:T(8,128)(2,1)}) custom-call(f32[16,256]{1,0:T(8,128)S(1)} %get-tuple-element.47.refs_0_, bf16[144,256]{1,0:T(8,128)(2,1)S(1)} %collective-permute-done.5.refs_6_.refs_1_, f32[16,256]{1,0:T(8,128)S(1)} %collective-permute-done.6.refs_2_, f32[16,256]{1,0:T(8,128)S(1)} %collective-permute-done.7.refs_3_, ...), custom_call_target="tpu_custom_call" | custom-call | tf_op jit(solution)/shard_map/finish/pallas_call | solution.py:242
  (2 shorter events, 0.1 us)
Async XLA Ops:
  0.6 7.0 %collective-permute-start = (bf16[16,256]{1,0:T(8,128)(2,1)}, bf16[16,256]{1,0:T(8,128)(2,1)S(1)}, u32[]{:S(2)}, u32[]{:S(2)}) collective-permute-start(bf16[16,256]{1,0:T(8,128)(2,1)} %feat_in.1), channel_id=1, source_target_pairs={{16,0},{0,16},{17,1},{1,17},{18,2},{2,18},{19,3},{3,19},{20,4},{4,... | collective-permute-start | bytes 24584 | tf_op jit(solution)/shard_map/ppermute | solution.py:215
  3.7 5.6 %collective-permute-start.1 = (bf16[16,256]{1,0:T(8,128)(2,1)}, bf16[16,256]{1,0:T(8,128)(2,1)S(1)}, u32[]{:S(2)}, u32[]{:S(2)}) collective-permute-start(bf16[16,256]{1,0:T(8,128)(2,1)} %cot_in.1), channel_id=1, source_target_pairs={{0,8},{1,9},{2,10},{3,11},{4,12},{5,13},{6,14},{7,15},{8,0},{9,1},... | collective-permute-start | bytes 24584 | tf_op jit(solution)/shard_map/ppermute | solution.py:95
  9.3 4.2 %collective-permute-start.2 = (bf16[96,256]{1,0:T(8,128)(2,1)S(1)}, bf16[96,256]{1,0:T(8,128)(2,1)S(1)}, u32[]{:S(2)}, u32[]{:S(2)}) collective-permute-start(bf16[96,256]{1,0:T(8,128)(2,1)S(1)} %get-tuple-element.44), channel_id=1, source_target_pairs={{0,2},{1,3},{2,0},{3,1},{4,6},{5,7},{6,4},{7,5},{8,10},{9,11},{10,... | collective-permute-start | bytes 147464 | tf_op jit(solution)/shard_map/ppermute | solution.py:95
  10.8 3.7 %collective-permute-start.3 = (bf16[96,256]{1,0:T(8,128)(2,1)S(1)}, bf16[96,256]{1,0:T(8,128)(2,1)S(1)}, u32[]{:S(2)}, u32[]{:S(2)}) collective-permute-start(bf16[96,256]{1,0:T(8,128)(2,1)S(1)} %get-tuple-element.45), channel_id=1, source_target_pairs={{0,3},{1,2},{2,1},{3,0},{4,7},{5,6},{6,5},{7,4},{8,11},{9,10},{10,... | collective-permute-start | bytes 147464 | tf_op jit(solution)/shard_map/ppermute | solution.py:95
  10.8 3.7 %collective-permute-start.4 = (bf16[96,256]{1,0:T(8,128)(2,1)S(1)}, bf16[96,256]{1,0:T(8,128)(2,1)S(1)}, u32[]{:S(2)}, u32[]{:S(2)}) collective-permute-start(bf16[96,256]{1,0:T(8,128)(2,1)S(1)} %get-tuple-element.46), channel_id=1, source_target_pairs={{0,1},{1,0},{2,3},{3,2},{4,5},{5,4},{6,7},{7,6},{8,9},{9,8},{10,11... | collective-permute-start | bytes 147464 | tf_op jit(solution)/shard_map/ppermute | solution.py:95
  14.5 4.4 %collective-permute-start.5 = (bf16[144,256]{1,0:T(8,128)(2,1)S(1)}, bf16[144,256]{1,0:T(8,128)(2,1)S(1)}, u32[]{:S(2)}, u32[]{:S(2)}) collective-permute-start(bf16[144,256]{1,0:T(8,128)(2,1)S(1)} %get-tuple-element.48), channel_id=1, source_target_pairs={{0,4},{1,5},{2,6},{3,7},{4,0},{5,1},{6,2},{7,3},{8,12},{9,13},{10,... | collective-permute-start | bytes 221192 | tf_op jit(solution)/shard_map/ppermute | solution.py:95
  16.2 6.0 %collective-permute-start.6 = (f32[16,256]{1,0:T(8,128)S(1)}, f32[16,256]{1,0:T(8,128)S(1)}, u32[]{:S(2)}, u32[]{:S(2)}) collective-permute-start(f32[16,256]{1,0:T(8,128)S(1)} %get-tuple-element.49), channel_id=1, source_target_pairs={{0,12},{1,13},{2,14},{3,15},{4,8},{5,9},{6,10},{7,11},{8,4},{9,5},... | collective-permute-start | bytes 49160 | tf_op jit(solution)/shard_map/ppermute | solution.py:95
  17.8 4.6 %collective-permute-start.7 = (f32[16,256]{1,0:T(8,128)S(1)}, f32[16,256]{1,0:T(8,128)S(1)}, u32[]{:S(2)}, u32[]{:S(2)}) collective-permute-start(f32[16,256]{1,0:T(8,128)S(1)} %get-tuple-element.50), channel_id=1, source_target_pairs={{0,8},{1,9},{2,10},{3,11},{4,12},{5,13},{6,14},{7,15},{8,0},{9,1},... | collective-permute-start | bytes 49160 | tf_op jit(solution)/shard_map/ppermute | solution.py:95
  20.3 3.7 %collective-permute-start.8 = (bf16[16,256]{1,0:T(8,128)(2,1)S(1)}, bf16[16,256]{1,0:T(8,128)(2,1)S(1)}, u32[]{:S(2)}, u32[]{:S(2)}) collective-permute-start(bf16[16,256]{1,0:T(8,128)(2,1)S(1)} %bitcast.4), channel_id=1, source_target_pairs={{16,0},{0,16},{17,1},{1,17},{18,2},{2,18},{19,3},{3,19},{20,4},{4,... | collective-permute-start | bytes 24584 | tf_op jit(solution)/shard_map/ppermute | solution.py:215

commit v2 on v1

--- a/solution.py
+++ b/solution.py
@@ -16,6 +16,7 @@
 VMEM = pl.BlockSpec(memory_space=pltpu.VMEM)
 ANY = pl.BlockSpec(memory_space=pl.ANY)
 CHUNK = 1536
+PARTS = 3
 
 
 def dot(a, b, dims=NN):
@@ -73,17 +74,17 @@
 STEPS = (0, 2, 3, 1)
 
 
+def block(far, near, me):
+    return far * (NEAR * INNER) + (me >> 1) * 4 + near * 2 + (me & 1)
+
+
 def place(index):
-    return index // (NEAR * INNER), index // INNER % NEAR, index % INNER
+    return index // (NEAR * INNER), (index >> 1) & 1, ((index >> 2) & 1) * 2 + (index & 1)
 
 
 def here():
     me = lax.axis_index("dst")
-    return lax.div(me, NEAR * INNER), lax.rem(lax.div(me, INNER), NEAR), lax.rem(me, INNER)
-
-
-def layer_steps(n_far):
-    return [0, 1, *range(n_far * NEAR - 1, 1, -1)]
+    return lax.div(me, NEAR * INNER), (me >> 1) & 1, ((me >> 2) & 1) * 2 + (me & 1)
 
 
 def layer_partner(far, near, n_far, k):
@@ -97,7 +98,7 @@
 
 def prepare(
     off_in, cnt_in, rel_in, sid_in, attr_in, cot_in, feat_in, bias_in, w_node_in, w_edge_in, w_out_in,
-    rows_out, dst_out, src_out, cot_out, feat_out, bias_out, w_node_out, w_edge_out,
+    rows_out, dst_out, turned_out, src_out, cot_out, feat_out, bias_out, w_node_out, w_edge_out,
     w_out_out, off, cnt, rel, sid, sems,
 ):
     width = attr_in.shape[1]
@@ -109,12 +110,13 @@
         sems,
     )
     wait(copies[:4])
-    spare = rows_out.shape[1] - width - 2 * src_out.shape[0]
+    spare = rows_out.shape[1] - width - PARTS * src_out.shape[0]
     fill = [jnp.zeros((spare, rel.shape[1]), F32)] if spare else []
     for at, to_dst, to_src in edge_hots(off, cnt, rel, sid, dst_out.shape[0], src_out.shape[0]):
         dst_out[:, at] = to_dst.astype(BF16)
+        turned_out[at, :] = to_dst.T.astype(BF16)
         src_out[:, at] = to_src.astype(BF16)
-        rows_out[at, width:] = jnp.concatenate([to_src, to_src, *fill], axis=0).T.astype(BF16)
+        rows_out[at, width:] = jnp.concatenate([to_src] * PARTS + fill, axis=0).T.astype(BF16)
     wait(copies[4:])
 
 
@@ -123,13 +125,16 @@
     me, owned = lax.axis_index("src"), feats[0].shape[0]
     for k, ref in enumerate(feats):
         group[part(lax.rem(me + k, n_src), owned), :] = ref[...]
-    high, low = halves(0.5 * (dot(group[...], w_node[...]) + bias[...]))
-    width, sources = w_edge.shape[0], group.shape[0]
-    first[:width, :] = 0.5 * w_edge[...]
-    first[width : width + sources, :] = high
-    first[width + sources : width + 2 * sources, :] = low
-    if first.shape[0] > width + 2 * sources:
-        first[width + 2 * sources :, :] = jnp.zeros_like(first[width + 2 * sources :, :])
+    table = 0.5 * (dot(group[...], w_node[...]) + bias[...])
+    first[: w_edge.shape[0], :] = 0.5 * w_edge[...]
+    end = w_edge.shape[0]
+    for _ in range(PARTS):
+        piece = table.astype(BF16)
+        first[end : end + group.shape[0], :] = piece
+        table = table - piece.astype(F32)
+        end += group.shape[0]
+    if first.shape[0] > end:
+        first[end:, :] = jnp.zeros_like(first[end:, :])
     for c in chunks(rows.shape[0]):
         half = dot(rows[c, :], first[...])
         half_out[c, :] = half
@@ -147,8 +152,9 @@
     for k, out in enumerate([keep, *sends]):
         to = partner(me, INNER, STEPS[k])
         for z in range(n_far * NEAR):
-            block = sums[part(z * INNER + to, owned), :]
-            out[z * owned : (z + 1) * owned, :] = block.astype(out.dtype)
+            whose = jnp.where(z // NEAR == far, to, to ^ 1)
+            its = sums[part(block(z // NEAR, z % NEAR, whose), owned), :]
+            out[z * owned : (z + 1) * owned, :] = its.astype(out.dtype)
         if k:
             out[rows:, :] = cots_out[...]
 
@@ -160,18 +166,19 @@
     for k, ref in enumerate([cots] + [ref.at[rows:, :] for ref in parts]):
         owner = partner(me, INNER, STEPS[k], True)
         for f in range(n_far):
-            block = ref[f * owned : (f + 1) * owned, :]
-            cots_out[part(f * INNER + owner, owned), :] = block
+            whose = jnp.where(f == far, owner, owner ^ 1)
+            cots_out[part(f * INNER + whose, owned), :] = ref[f * owned : (f + 1) * owned, :]
     total[...] = sum((ref[:rows, :].astype(F32) for ref in parts), keep[...])
     for k, out in enumerate([own, *sends]):
-        layer = layer_partner(far, near, n_far, layer_steps(n_far)[k])
+        layer = layer_partner(far, near, n_far, k)
         out[:owned, :] = total[part(layer, owned), :].astype(out.dtype)
     sends[0][owned:, :] = cots_out[...]
 
 
-def slopes(_, half, dst_hot, slope_out, turned_out):
+def slopes(_, half, w_node, w_out, slope_out, w_node_out, w_out_out):
+    w_out_out[...] = w_out[...].T
+    w_node_out[...] = w_node[...].T
     for c in chunks(half.shape[0]):
-        turned_out[c, :] = dst_hot[:, c].astype(F32).T.astype(BF16)
         t = jnp.tanh(half[c, :])
         slope_out[c, :] = 0.5 + 0.5 * (t + half[c, :] * (1.0 - t * t))
 
@@ -181,17 +188,17 @@
     d_pre, keep_out, send_out, total, cots,
 ):
     _, near, _ = here()
-    owned, run = keep_out.shape[0], INNER * keep_out.shape[0]
-    for f in range(cots_near.shape[0] // run):
-        at = f * run
-        cots[part(f * NEAR + near, run), :] = cots_near[at : at + run, :]
+    owned, run = keep_out.shape[0], 2 * keep_out.shape[0]
+    for pair in range(cots_near.shape[0] // run):
+        at = pair * run
+        cots[part(pair * NEAR + near, run), :] = cots_near[at : at + run, :]
         at += owned
-        cots[part(f * NEAR + 1 - near, run), :] = came[at : at + run, :]
+        cots[part(pair * NEAR + 1 - near, run), :] = came[at : at + run, :]
     for c in chunks(slope.shape[0]):
         d_message = dot(dst_hot[c, :], cots[...]).astype(BF16)
-        d_pre[c, :] = (dot(d_message, w_out[...], NT) * slope[c, :]).astype(BF16)
+        d_pre[c, :] = (dot(d_message, w_out[...]) * slope[c, :]).astype(BF16)
     high, low = halves(dot(src_hot[...], d_pre[...]))
-    total[...] = dot(high, w_node[...], NT) + dot(low, w_node[...], NT)
+    total[...] = dot(high, w_node[...]) + dot(low, w_node[...])
     me = lax.axis_index("src")
     keep_out[...] = total[part(me, owned), :]
     for k in range(1, n_src):
@@ -252,16 +259,17 @@
     ints = [offsets, counts, dst_rel.reshape(blocks, width), src_ids.reshape(blocks, width)]
     bias = bias.reshape(1, hidden)
     feats = [ahead(node_feats, "src", k) for k in range(1, n_src)]
-    depth = attr_width + 2 * src_rows
+    depth = attr_width + PARTS * src_rows
     depth += -depth % 128
 
-    rows, dst_hot, src_hot, cots, own, *params_near = call(
+    rows, dst_hot, turned, src_hot, cots, own, *params_near = call(
         prepare,
         "prepare",
         [in_hbm(x) for x in (*ints, edge_attr, cotangent, node_feats, bias, w_node, w_edge, w_out)],
         [
             array(edges, depth),
             array(dst_rows, edges),
+            array(edges, dst_rows),
             array(src_rows, edges),
             rows_of(1),
             rows_of(1),
@@ -276,7 +284,8 @@
     _, w_node, w_edge, w_out = params_near
 
     def to_far(i, k):
-        return i + (partner_of(place(i)[0], n_far, k) - place(i)[0]) * NEAR * INNER
+        far, near, me = place(i)
+        return block(partner_of(far, n_far, k), near, me ^ 1)
 
     parts = swap([cotangent] * (n_far - 1), to_far)
 
@@ -298,13 +307,17 @@
         [sums, cots, *parts],
         [rows_of(n_far), rows_of(layers, F32)] + [rows_of(layers + n_far)] * (INNER - 1),
     )
-    parts = swap(sends, lambda i, k: i - i % INNER + partner_of(i % INNER, INNER, STEPS[k]))
-
-    slope, turned = call(
+    def to_inner(i, k):
+        far, near, me = place(i)
+        return block(far, near, partner_of(me, INNER, STEPS[k]))
+
+    parts = swap(sends, to_inner)
+
+    slope, w_node, w_out = call(
         slopes,
         "slopes",
-        [keep, half, dst_hot],
-        [array(edges, hidden, dtype=F32), array(edges, dst_rows)],
+        [keep, half, w_node, w_out],
+        [array(edges, hidden, dtype=F32)] + [array(*x.shape[::-1]) for x in (w_node, w_out)],
     )
 
     beside = n_far * INNER
@@ -319,9 +332,8 @@
 
     def to_layer(i, k):
         far, near, me = place(i)
-        k = layer_steps(n_far)[k]
-        to = partner_of(far, n_far, k // NEAR) * NEAR + partner_of(near, NEAR, k % NEAR)
-        return to * INNER + me
+        far, near = partner_of(far, n_far, k // NEAR), partner_of(near, NEAR, k % NEAR)
+        return block(far, near, me ^ (k >= NEAR))
 
     parts = swap(sends, to_layer)
 

time: 24.7 us -> 24.3 us (0.984)
  waiting for transfers between devices: 3.92 us -> 3.65 us
    ppermute x7, waiting for transfers between devices: 2.44 us -> 1.83 us  [swap(): return [lax.ppermute(x, 'dst', pairs[k + 1]) for k, x in enumerate(sends)]]
    ppermute x2, waiting for transfers between devices: 1.48 us -> 1.82 us  [ahead(): return lax.ppermute(x, axis, [((i + k) % n, i) for i in range(n)])]
  transfers between devices with their start and end apart: 9 -> 9, of which waited for: 5 -> 4; matrix products, arithmetic and copies ran while one was open for 0% -> 0% of each run, Pallas kernels for 30% -> 30%
where the time goes in v2:
time: 24.3 us; the launch traced here: 24.1 us
  starting transfers between devices  11.9 us (49%)
  Pallas kernels  7.91 us (33%)
  waiting for transfers between devices  3.65 us (15%)
  between operations  0.7 us (3%)
    ppermute x7, starting transfers between devices, swap(): return [lax.ppermute(x, 'dst', pairs[k + 1]) for k, x in enumerate(sends)]  8.31 us
    pallas_call x8, Pallas kernels, call(): pl.pallas_call(kernel, name=name, in_specs=specs or [VMEM] * len(args), o...  7.91 us
    ppermute x2, starting transfers between devices, ahead(): return lax.ppermute(x, axis, [((i + k) % n, i) for i in range(n)])  3.56 us
    ppermute x7, waiting for transfers between devices, swap(): return [lax.ppermute(x, 'dst', pairs[k + 1]) for k, x in enumerate(sends)]  1.83 us
    ppermute x2, waiting for transfers between devices, ahead(): return lax.ppermute(x, axis, [((i + k) % n, i) for i in range(n)])  1.82 us
  transfers between devices with their start and end apart: 9, of which 4 were waited for; matrix products, arithmetic and copies ran while one was open for 0% of the time, Pallas kernels for 30%

profile of v2, /device:TPU:0, one launch (start us, length us, event | category | flops | bytes accessed | tf_op | source)
XLA Modules:
  0.0 24.1 jit_solution(4904261279333417731)
XLA Ops:
  0.6 3.0 %collective-permute-start = (bf16[16,256]{1,0:T(8,128)(2,1)}, bf16[16,256]{1,0:T(8,128)(2,1)S(1)}, u32[]{:S(2)}, u32[]{:S(2)}) collective-permute-start(bf16[16,256]{1,0:T(8,128)(2,1)} %feat_in.1), channel_id=1, source_target_pairs={{16,0},{0,16},{17,1},{1,17},{18,2},{2,18},{19,3},{3,19},{20,4},{4,... | collective-permute-start | bytes 24584 | tf_op jit(solution)/shard_map/ppermute | solution.py:222
  3.7 1.7 %collective-permute-start.1 = (bf16[16,256]{1,0:T(8,128)(2,1)}, bf16[16,256]{1,0:T(8,128)(2,1)S(1)}, u32[]{:S(2)}, u32[]{:S(2)}) collective-permute-start(bf16[16,256]{1,0:T(8,128)(2,1)} %cot_in.1), channel_id=1, source_target_pairs={{0,9},{1,8},{2,11},{3,10},{4,13},{5,12},{6,15},{7,14},{8,1},{9,0},... | collective-permute-start | bytes 24584 | tf_op jit(solution)/shard_map/ppermute | solution.py:96
  5.4 1.4 %prepare.1 = (bf16[1536,256]{1,0:T(8,128)(2,1)S(1)}, bf16[256,1536]{1,0:T(8,128)(2,1)S(1)}, bf16[1536,256]{1,0:T(8,128)(2,1)S(1)}, bf16[32,1536]{1,0:T(8,128)(2,...) custom-call(s32[12]{0:T(128)} %off_in.1, ...), custom_call_target="tpu_custom_call" | custom-call | tf_op jit(solution)/shard_map/prepare/pallas_call | solution.py:249
  6.8 0.0 collective-permute-done.refs_7_
  6.8 1.5 %forward.1 = (f32[1536,512]{1,0:T(8,128)S(1)}, f32[256,256]{1,0:T(8,128)S(1)}) custom-call(bf16[1536,256]{1,0:T(8,128)(2,1)S(1)} %get-tuple-element.33.refs_0_, bf16[256,1536]{1,0:T(8,128)(2,1)S(1)} %get-tuple-element.34.refs_1_, f32[1,512]{1,0:T(1,128)S(1)} %get-tuple-element.35.refs_2_, bf16[256,512]{1,0:T(8,128)(2,1)S(1)} %get-tuple-element.36.refs_3_.w_node, ...), custom_call_target="tpu_custom_call" | custom-call | tf_op jit(solution)/shard_map/forward/pallas_call | solution.py:249
  8.4 0.0 collective-permute-done.1.refs_2_
  8.4 0.1 pack.1
  8.4 1.6 %collective-permute-start.2 = (bf16[96,256]{1,0:T(8,128)(2,1)S(1)}, bf16[96,256]{1,0:T(8,128)(2,1)S(1)}, u32[]{:S(2)}, u32[]{:S(2)}) collective-permute-start(bf16[96,256]{1,0:T(8,128)(2,1)S(1)} %get-tuple-element.46), channel_id=1, source_target_pairs={{0,4},{1,5},{2,6},{3,7},{4,0},{5,1},{6,2},{7,3},{8,12},{9,13},{10,... | collective-permute-start | bytes 147464 | tf_op jit(solution)/shard_map/ppermute | solution.py:96
  10.1 0.7 %collective-permute-start.3 = (bf16[96,256]{1,0:T(8,128)(2,1)S(1)}, bf16[96,256]{1,0:T(8,128)(2,1)S(1)}, u32[]{:S(2)}, u32[]{:S(2)}) collective-permute-start(bf16[96,256]{1,0:T(8,128)(2,1)S(1)} %get-tuple-element.47), channel_id=1, source_target_pairs={{0,5},{1,4},{2,7},{3,6},{4,1},{5,0},{6,3},{7,2},{8,13},{9,12},{10,... | collective-permute-start | bytes 147464 | tf_op jit(solution)/shard_map/ppermute | solution.py:96
  10.8 0.0 collective-permute-start.4
  10.8 1.7 %slopes.1 = (f32[1536,512]{1,0:T(8,128)S(1)}, bf16[512,256]{1,0:T(8,128)(2,1)S(1)}, bf16[256,512]{1,0:T(8,128)(2,1)S(1)}) custom-call(f32[64,256]{1,0:T(8,128)S(1)} %get-tuple-element.42._.refs_2_, f32[1536,512]{1,0:T(8,128)S(1)} %get-tuple-element.43.half, bf16[256,512]{1,0:T(8,128)(2,1)S(1)} %get-tuple-element.36.refs_3_.w_node, ...), custom_call_target="tpu_custom_call" | custom-call | tf_op jit(solution)/shard_map/slopes/pallas_call | solution.py:249
  12.5 0.6 %collective-permute-done.2.refs_3_ = bf16[96,256]{1,0:T(8,128)(2,1)S(1)} collective-permute-done((bf16[96,256]{1,0:T(8,128)(2,1)S(1)}, bf16[96,256]{1,0:T(8,128)(2,1)S(1)}, u32[]{:S(2)}, u32[]{:S(2)}) %collective-permute-start.2) | collective-permute-done | bytes 49184 | tf_op jit(solution)/shard_map/ppermute | solution.py:96
  13.1 0.5 %collective-permute-done.3.refs_4_ = bf16[96,256]{1,0:T(8,128)(2,1)S(1)} collective-permute-done((bf16[96,256]{1,0:T(8,128)(2,1)S(1)}, bf16[96,256]{1,0:T(8,128)(2,1)S(1)}, u32[]{:S(2)}, u32[]{:S(2)}) %collective-permute-start.3) | collective-permute-done | bytes 49184 | tf_op jit(solution)/shard_map/ppermute | solution.py:96
  13.6 0.0 collective-permute-done.4.refs_5_
  13.7 1.6 %collective-permute-start.5 = (bf16[144,256]{1,0:T(8,128)(2,1)S(1)}, bf16[144,256]{1,0:T(8,128)(2,1)S(1)}, u32[]{:S(2)}, u32[]{:S(2)}) collective-permute-start(bf16[144,256]{1,0:T(8,128)(2,1)S(1)} %get-tuple-element.50), channel_id=1, source_target_pairs={{0,2},{1,3},{2,0},{3,1},{4,6},{5,7},{6,4},{7,5},{8,10},{9,11},{10,... | collective-permute-start | bytes 221192 | tf_op jit(solution)/shard_map/ppermute | solution.py:96
  15.2 1.0 %collective-permute-start.6 = (f32[16,256]{1,0:T(8,128)S(1)}, f32[16,256]{1,0:T(8,128)S(1)}, u32[]{:S(2)}, u32[]{:S(2)}) collective-permute-start(f32[16,256]{1,0:T(8,128)S(1)} %get-tuple-element.51), channel_id=1, source_target_pairs={{0,9},{1,8},{2,11},{3,10},{4,13},{5,12},{6,15},{7,14},{8,1},{9,0},... | collective-permute-start | bytes 49160 | tf_op jit(solution)/shard_map/ppermute | solution.py:96
  16.3 1.6 %collective-permute-start.7 = (f32[16,256]{1,0:T(8,128)S(1)}, f32[16,256]{1,0:T(8,128)S(1)}, u32[]{:S(2)}, u32[]{:S(2)}) collective-permute-start(f32[16,256]{1,0:T(8,128)S(1)} %get-tuple-element.52), channel_id=1, source_target_pairs={{0,11},{1,10},{2,9},{3,8},{4,15},{5,14},{6,13},{7,12},{8,3},{9,2},... | collective-permute-start | bytes 49160 | tf_op jit(solution)/shard_map/ppermute | solution.py:96
  17.9 0.7 %collective-permute-done.5.refs_6_.refs_1_ = bf16[144,256]{1,0:T(8,128)(2,1)S(1)} collective-permute-done((bf16[144,256]{1,0:T(8,128)(2,1)S(1)}, bf16[144,256]{1,0:T(8,128)(2,1)S(1)}, u32[]{:S(2)}, u32[]{:S(2)}) %collective-permute-start.5) | collective-permute-done | bytes 73760 | tf_op jit(solution)/shard_map/ppermute | solution.py:96
  18.6 1.3 %backward.1 = (bf16[1536,512]{1,0:T(8,128)(2,1)S(1)}, f32[16,256]{1,0:T(8,128)S(1)}, bf16[1,16,256]{2,1,0:T(8,128)(2,1)S(1)}) custom-call(f32[1536,512]{1,0:T(8,128)S(1)} %get-tuple-element.44.refs_0_, bf16[1536,256]{1,0:T(8,128)(2,1)S(1)} %get-tuple-element.53.refs_1_, bf16[32,1536]{1,0:T(8,128)(2,1)S(1)} %get-tuple-element.54.refs_2_, ...), custom_call_target="tpu_custom_call" | custom-call | tf_op jit(solution)/shard_map/backward/pallas_call | solution.py:249
  19.8 0.5 %collective-permute-start.8 = (bf16[16,256]{1,0:T(8,128)(2,1)S(1)}, bf16[16,256]{1,0:T(8,128)(2,1)S(1)}, u32[]{:S(2)}, u32[]{:S(2)}) collective-permute-start(bf16[16,256]{1,0:T(8,128)(2,1)S(1)} %bitcast.4), channel_id=1, source_target_pairs={{16,0},{0,16},{17,1},{1,17},{18,2},{2,18},{19,3},{3,19},{20,4},{4,... | collective-permute-start | bytes 24584 | tf_op jit(solution)/shard_map/ppermute | solution.py:222
  20.4 1.3 %attributes.1 = bf16[1536,128]{1,0:T(8,128)(2,1)} custom-call(bf16[1536,512]{1,0:T(8,128)(2,1)S(1)} %get-tuple-element.62.d_pre, bf16[128,512]{1,0:T(8,128)(2,1)S(1)} %get-tuple-element.37.refs_4_.w_edge), custom_call_target="tpu_custom_call" | custom-call | tf_op jit(solution)/shard_map/attributes/pallas_call | solution.py:249
  21.7 0.0 collective-permute-done.6.refs_2_
  21.7 0.0 collective-permute-done.7.refs_3_
  21.7 1.8 %collective-permute-done.8.refs_5_ = bf16[16,256]{1,0:T(8,128)(2,1)S(1)} collective-permute-done((bf16[16,256]{1,0:T(8,128)(2,1)S(1)}, bf16[16,256]{1,0:T(8,128)(2,1)S(1)}, u32[]{:S(2)}, u32[]{:S(2)}) %collective-permute-start.8) | collective-permute-done | bytes 8224 | tf_op jit(solution)/shard_map/ppermute | solution.py:222
  23.5 0.6 %finish.1 = (bf16[16,256]{1,0:T(8,128)(2,1)}, bf16[16,256]{1,0:T(8,128)(2,1)}) custom-call(f32[16,256]{1,0:T(8,128)S(1)} %get-tuple-element.49.refs_0_, bf16[144,256]{1,0:T(8,128)(2,1)S(1)} %collective-permute-done.5.refs_6_.refs_1_, f32[16,256]{1,0:T(8,128)S(1)} %collective-permute-done.6.refs_2_, f32[16,256]{1,0:T(8,128)S(1)} %collective-permute-done.7.refs_3_, ...), custom_call_target="tpu_custom_call" | custom-call | tf_op jit(solution)/shard_map/finish/pallas_call | solution.py:249
  (1 shorter events, 0.0 us)
Async XLA Ops:
  0.6 6.2 %collective-permute-start = (bf16[16,256]{1,0:T(8,128)(2,1)}, bf16[16,256]{1,0:T(8,128)(2,1)S(1)}, u32[]{:S(2)}, u32[]{:S(2)}) collective-permute-start(bf16[16,256]{1,0:T(8,128)(2,1)} %feat_in.1), channel_id=1, source_target_pairs={{16,0},{0,16},{17,1},{1,17},{18,2},{2,18},{19,3},{3,19},{20,4},{4,... | collective-permute-start | bytes 24584 | tf_op jit(solution)/shard_map/ppermute | solution.py:222
  3.7 4.7 %collective-permute-start.1 = (bf16[16,256]{1,0:T(8,128)(2,1)}, bf16[16,256]{1,0:T(8,128)(2,1)S(1)}, u32[]{:S(2)}, u32[]{:S(2)}) collective-permute-start(bf16[16,256]{1,0:T(8,128)(2,1)} %cot_in.1), channel_id=1, source_target_pairs={{0,9},{1,8},{2,11},{3,10},{4,13},{5,12},{6,15},{7,14},{8,1},{9,0},... | collective-permute-start | bytes 24584 | tf_op jit(solution)/shard_map/ppermute | solution.py:96
  8.4 4.7 %collective-permute-start.2 = (bf16[96,256]{1,0:T(8,128)(2,1)S(1)}, bf16[96,256]{1,0:T(8,128)(2,1)S(1)}, u32[]{:S(2)}, u32[]{:S(2)}) collective-permute-start(bf16[96,256]{1,0:T(8,128)(2,1)S(1)} %get-tuple-element.46), channel_id=1, source_target_pairs={{0,4},{1,5},{2,6},{3,7},{4,0},{5,1},{6,2},{7,3},{8,12},{9,13},{10,... | collective-permute-start | bytes 147464 | tf_op jit(solution)/shard_map/ppermute | solution.py:96
  10.1 3.6 %collective-permute-start.3 = (bf16[96,256]{1,0:T(8,128)(2,1)S(1)}, bf16[96,256]{1,0:T(8,128)(2,1)S(1)}, u32[]{:S(2)}, u32[]{:S(2)}) collective-permute-start(bf16[96,256]{1,0:T(8,128)(2,1)S(1)} %get-tuple-element.47), channel_id=1, source_target_pairs={{0,5},{1,4},{2,7},{3,6},{4,1},{5,0},{6,3},{7,2},{8,13},{9,12},{10,... | collective-permute-start | bytes 147464 | tf_op jit(solution)/shard_map/ppermute | solution.py:96
  10.8 2.8 %collective-permute-start.4 = (bf16[96,256]{1,0:T(8,128)(2,1)S(1)}, bf16[96,256]{1,0:T(8,128)(2,1)S(1)}, u32[]{:S(2)}, u32[]{:S(2)}) collective-permute-start(bf16[96,256]{1,0:T(8,128)(2,1)S(1)} %get-tuple-element.48), channel_id=1, source_target_pairs={{0,1},{1,0},{2,3},{3,2},{4,5},{5,4},{6,7},{7,6},{8,9},{9,8},{10,11... | collective-permute-start | bytes 147464 | tf_op jit(solution)/shard_map/ppermute | solution.py:96
  13.7 4.9 %collective-permute-start.5 = (bf16[144,256]{1,0:T(8,128)(2,1)S(1)}, bf16[144,256]{1,0:T(8,128)(2,1)S(1)}, u32[]{:S(2)}, u32[]{:S(2)}) collective-permute-start(bf16[144,256]{1,0:T(8,128)(2,1)S(1)} %get-tuple-element.50), channel_id=1, source_target_pairs={{0,2},{1,3},{2,0},{3,1},{4,6},{5,7},{6,4},{7,5},{8,10},{9,11},{10,... | collective-permute-start | bytes 221192 | tf_op jit(solution)/shard_map/ppermute | solution.py:96
  15.2 6.4 %collective-permute-start.6 = (f32[16,256]{1,0:T(8,128)S(1)}, f32[16,256]{1,0:T(8,128)S(1)}, u32[]{:S(2)}, u32[]{:S(2)}) collective-permute-start(f32[16,256]{1,0:T(8,128)S(1)} %get-tuple-element.51), channel_id=1, source_target_pairs={{0,9},{1,8},{2,11},{3,10},{4,13},{5,12},{6,15},{7,14},{8,1},{9,0},... | collective-permute-start | bytes 49160 | tf_op jit(solution)/shard_map/ppermute | solution.py:96
  16.3 5.4 %collective-permute-start.7 = (f32[16,256]{1,0:T(8,128)S(1)}, f32[16,256]{1,0:T(8,128)S(1)}, u32[]{:S(2)}, u32[]{:S(2)}) collective-permute-start(f32[16,256]{1,0:T(8,128)S(1)} %get-tuple-element.52), channel_id=1, source_target_pairs={{0,11},{1,10},{2,9},{3,8},{4,15},{5,14},{6,13},{7,12},{8,3},{9,2},... | collective-permute-start | bytes 49160 | tf_op jit(solution)/shard_map/ppermute | solution.py:96
  19.8 3.7 %collective-permute-start.8 = (bf16[16,256]{1,0:T(8,128)(2,1)S(1)}, bf16[16,256]{1,0:T(8,128)(2,1)S(1)}, u32[]{:S(2)}, u32[]{:S(2)}) collective-permute-start(bf16[16,256]{1,0:T(8,128)(2,1)S(1)} %bitcast.4), channel_id=1, source_target_pairs={{16,0},{0,16},{17,1},{1,17},{18,2},{2,18},{19,3},{3,19},{20,4},{4,... | collective-permute-start | bytes 24584 | tf_op jit(solution)/shard_map/ppermute | solution.py:222

commit v3 on v2

--- a/solution.py
+++ b/solution.py
@@ -152,7 +152,7 @@
     for k, out in enumerate([keep, *sends]):
         to = partner(me, INNER, STEPS[k])
         for z in range(n_far * NEAR):
-            whose = jnp.where(z // NEAR == far, to, to ^ 1)
+            whose = jnp.where(z == far * NEAR + near, to, to ^ 1)
             its = sums[part(block(z // NEAR, z % NEAR, whose), owned), :]
             out[z * owned : (z + 1) * owned, :] = its.astype(out.dtype)
         if k:
@@ -333,7 +333,7 @@
     def to_layer(i, k):
         far, near, me = place(i)
         far, near = partner_of(far, n_far, k // NEAR), partner_of(near, NEAR, k % NEAR)
-        return block(far, near, me ^ (k >= NEAR))
+        return block(far, near, me ^ 1)
 
     parts = swap(sends, to_layer)
 

time: 24.3 us -> 23.8 us (0.979)
  waiting for transfers between devices: 3.65 us -> 2.97 us
    ppermute x2, waiting for transfers between devices: 1.82 us -> 1.08 us  [ahead(): return lax.ppermute(x, axis, [((i + k) % n, i) for i in range(n)])]
where the time goes in v3:
time: 23.8 us; the launch traced here: 23.7 us
  starting transfers between devices  12.1 us (51%)
  Pallas kernels  7.92 us (33%)
  waiting for transfers between devices  2.97 us (12%)
  between operations  0.7 us (3%)
    ppermute x7, starting transfers between devices, swap(): return [lax.ppermute(x, 'dst', pairs[k + 1]) for k, x in enumerate(sends)]  8.54 us
    pallas_call x8, Pallas kernels, call(): pl.pallas_call(kernel, name=name, in_specs=specs or [VMEM] * len(args), o...  7.92 us
    ppermute x2, starting transfers between devices, ahead(): return lax.ppermute(x, axis, [((i + k) % n, i) for i in range(n)])  3.56 us
    ppermute x7, waiting for transfers between devices, swap(): return [lax.ppermute(x, 'dst', pairs[k + 1]) for k, x in enumerate(sends)]  1.89 us
    ppermute x2, waiting for transfers between devices, ahead(): return lax.ppermute(x, axis, [((i + k) % n, i) for i in range(n)])  1.08 us
  transfers between devices with their start and end apart: 9, of which 4 were waited for; matrix products, arithmetic and copies ran while one was open for 0% of the time, Pallas kernels for 30%

profile of v3, /device:TPU:0, one launch (start us, length us, event | category | flops | bytes accessed | tf_op | source)
XLA Modules:
  0.0 23.7 jit_solution(8504826971566856646)
XLA Ops:
  0.6 3.0 %collective-permute-start = (bf16[16,256]{1,0:T(8,128)(2,1)}, bf16[16,256]{1,0:T(8,128)(2,1)S(1)}, u32[]{:S(2)}, u32[]{:S(2)}) collective-permute-start(bf16[16,256]{1,0:T(8,128)(2,1)} %feat_in.1), channel_id=1, source_target_pairs={{16,0},{0,16},{17,1},{1,17},{18,2},{2,18},{19,3},{3,19},{20,4},{4,... | collective-permute-start | bytes 24584 | tf_op jit(solution)/shard_map/ppermute | solution.py:222
  3.7 1.7 %collective-permute-start.1 = (bf16[16,256]{1,0:T(8,128)(2,1)}, bf16[16,256]{1,0:T(8,128)(2,1)S(1)}, u32[]{:S(2)}, u32[]{:S(2)}) collective-permute-start(bf16[16,256]{1,0:T(8,128)(2,1)} %cot_in.1), channel_id=1, source_target_pairs={{0,9},{1,8},{2,11},{3,10},{4,13},{5,12},{6,15},{7,14},{8,1},{9,0},... | collective-permute-start | bytes 24584 | tf_op jit(solution)/shard_map/ppermute | solution.py:96
  5.4 1.4 %prepare.1 = (bf16[1536,256]{1,0:T(8,128)(2,1)S(1)}, bf16[256,1536]{1,0:T(8,128)(2,1)S(1)}, bf16[1536,256]{1,0:T(8,128)(2,1)S(1)}, bf16[32,1536]{1,0:T(8,128)(2,...) custom-call(s32[12]{0:T(128)} %off_in.1, ...), custom_call_target="tpu_custom_call" | custom-call | tf_op jit(solution)/shard_map/prepare/pallas_call | solution.py:249
  6.8 0.0 collective-permute-done.refs_7_
  6.8 1.5 %forward.1 = (f32[1536,512]{1,0:T(8,128)S(1)}, f32[256,256]{1,0:T(8,128)S(1)}) custom-call(bf16[1536,256]{1,0:T(8,128)(2,1)S(1)} %get-tuple-element.33.refs_0_, bf16[256,1536]{1,0:T(8,128)(2,1)S(1)} %get-tuple-element.34.refs_1_, f32[1,512]{1,0:T(1,128)S(1)} %get-tuple-element.35.refs_2_, bf16[256,512]{1,0:T(8,128)(2,1)S(1)} %get-tuple-element.36.refs_3_.w_node, ...), custom_call_target="tpu_custom_call" | custom-call | tf_op jit(solution)/shard_map/forward/pallas_call | solution.py:249
  8.4 0.0 collective-permute-done.1.refs_2_
  8.4 0.1 pack.1
  8.5 1.6 %collective-permute-start.2 = (bf16[96,256]{1,0:T(8,128)(2,1)S(1)}, bf16[96,256]{1,0:T(8,128)(2,1)S(1)}, u32[]{:S(2)}, u32[]{:S(2)}) collective-permute-start(bf16[96,256]{1,0:T(8,128)(2,1)S(1)} %get-tuple-element.46), channel_id=1, source_target_pairs={{0,4},{1,5},{2,6},{3,7},{4,0},{5,1},{6,2},{7,3},{8,12},{9,13},{10,... | collective-permute-start | bytes 147464 | tf_op jit(solution)/shard_map/ppermute | solution.py:96
  10.1 0.7 %collective-permute-start.3 = (bf16[96,256]{1,0:T(8,128)(2,1)S(1)}, bf16[96,256]{1,0:T(8,128)(2,1)S(1)}, u32[]{:S(2)}, u32[]{:S(2)}) collective-permute-start(bf16[96,256]{1,0:T(8,128)(2,1)S(1)} %get-tuple-element.47), channel_id=1, source_target_pairs={{0,5},{1,4},{2,7},{3,6},{4,1},{5,0},{6,3},{7,2},{8,13},{9,12},{10,... | collective-permute-start | bytes 147464 | tf_op jit(solution)/shard_map/ppermute | solution.py:96
  10.8 0.0 collective-permute-start.4
  10.8 1.7 %slopes.1 = (f32[1536,512]{1,0:T(8,128)S(1)}, bf16[512,256]{1,0:T(8,128)(2,1)S(1)}, bf16[256,512]{1,0:T(8,128)(2,1)S(1)}) custom-call(f32[64,256]{1,0:T(8,128)S(1)} %get-tuple-element.42._.refs_2_, f32[1536,512]{1,0:T(8,128)S(1)} %get-tuple-element.43.half, bf16[256,512]{1,0:T(8,128)(2,1)S(1)} %get-tuple-element.36.refs_3_.w_node, ...), custom_call_target="tpu_custom_call" | custom-call | tf_op jit(solution)/shard_map/slopes/pallas_call | solution.py:249
  12.5 0.6 %collective-permute-done.2.refs_3_ = bf16[96,256]{1,0:T(8,128)(2,1)S(1)} collective-permute-done((bf16[96,256]{1,0:T(8,128)(2,1)S(1)}, bf16[96,256]{1,0:T(8,128)(2,1)S(1)}, u32[]{:S(2)}, u32[]{:S(2)}) %collective-permute-start.2) | collective-permute-done | bytes 49184 | tf_op jit(solution)/shard_map/ppermute | solution.py:96
  13.1 0.5 %collective-permute-done.3.refs_4_ = bf16[96,256]{1,0:T(8,128)(2,1)S(1)} collective-permute-done((bf16[96,256]{1,0:T(8,128)(2,1)S(1)}, bf16[96,256]{1,0:T(8,128)(2,1)S(1)}, u32[]{:S(2)}, u32[]{:S(2)}) %collective-permute-start.3) | collective-permute-done | bytes 49184 | tf_op jit(solution)/shard_map/ppermute | solution.py:96
  13.7 0.0 collective-permute-done.4.refs_5_
  13.7 1.8 %collective-permute-start.5 = (bf16[144,256]{1,0:T(8,128)(2,1)S(1)}, bf16[144,256]{1,0:T(8,128)(2,1)S(1)}, u32[]{:S(2)}, u32[]{:S(2)}) collective-permute-start(bf16[144,256]{1,0:T(8,128)(2,1)S(1)} %get-tuple-element.50), channel_id=1, source_target_pairs={{0,3},{1,2},{2,1},{3,0},{4,7},{5,6},{6,5},{7,4},{8,11},{9,10},{10,... | collective-permute-start | bytes 221192 | tf_op jit(solution)/shard_map/ppermute | solution.py:96
  15.5 1.5 %collective-permute-start.6 = (f32[16,256]{1,0:T(8,128)S(1)}, f32[16,256]{1,0:T(8,128)S(1)}, u32[]{:S(2)}, u32[]{:S(2)}) collective-permute-start(f32[16,256]{1,0:T(8,128)S(1)} %get-tuple-element.51), channel_id=1, source_target_pairs={{0,9},{1,8},{2,11},{3,10},{4,13},{5,12},{6,15},{7,14},{8,1},{9,0},... | collective-permute-start | bytes 49160 | tf_op jit(solution)/shard_map/ppermute | solution.py:96
  17.0 1.1 %collective-permute-start.7 = (f32[16,256]{1,0:T(8,128)S(1)}, f32[16,256]{1,0:T(8,128)S(1)}, u32[]{:S(2)}, u32[]{:S(2)}) collective-permute-start(f32[16,256]{1,0:T(8,128)S(1)} %get-tuple-element.52), channel_id=1, source_target_pairs={{0,11},{1,10},{2,9},{3,8},{4,15},{5,14},{6,13},{7,12},{8,3},{9,2},... | collective-permute-start | bytes 49160 | tf_op jit(solution)/shard_map/ppermute | solution.py:96
  18.1 0.0 collective-permute-done.5.refs_6_.refs_1_
  18.1 1.3 %backward.1 = (bf16[1536,512]{1,0:T(8,128)(2,1)S(1)}, f32[16,256]{1,0:T(8,128)S(1)}, bf16[1,16,256]{2,1,0:T(8,128)(2,1)S(1)}) custom-call(f32[1536,512]{1,0:T(8,128)S(1)} %get-tuple-element.44.refs_0_, bf16[1536,256]{1,0:T(8,128)(2,1)S(1)} %get-tuple-element.53.refs_1_, bf16[32,1536]{1,0:T(8,128)(2,1)S(1)} %get-tuple-element.54.refs_2_, ...), custom_call_target="tpu_custom_call" | custom-call | tf_op jit(solution)/shard_map/backward/pallas_call | solution.py:249
  19.4 0.5 %collective-permute-start.8 = (bf16[16,256]{1,0:T(8,128)(2,1)S(1)}, bf16[16,256]{1,0:T(8,128)(2,1)S(1)}, u32[]{:S(2)}, u32[]{:S(2)}) collective-permute-start(bf16[16,256]{1,0:T(8,128)(2,1)S(1)} %bitcast.4), channel_id=1, source_target_pairs={{16,0},{0,16},{17,1},{1,17},{18,2},{2,18},{19,3},{3,19},{20,4},{4,... | collective-permute-start | bytes 24584 | tf_op jit(solution)/shard_map/ppermute | solution.py:222
  19.9 1.3 %attributes.1 = bf16[1536,128]{1,0:T(8,128)(2,1)} custom-call(bf16[1536,512]{1,0:T(8,128)(2,1)S(1)} %get-tuple-element.62.d_pre, bf16[128,512]{1,0:T(8,128)(2,1)S(1)} %get-tuple-element.37.refs_4_.w_edge), custom_call_target="tpu_custom_call" | custom-call | tf_op jit(solution)/shard_map/attributes/pallas_call | solution.py:249
  21.2 0.0 collective-permute-done.6.refs_2_
  21.2 0.7 %collective-permute-done.7.refs_3_ = f32[16,256]{1,0:T(8,128)S(1)} collective-permute-done((f32[16,256]{1,0:T(8,128)S(1)}, f32[16,256]{1,0:T(8,128)S(1)}, u32[]{:S(2)}, u32[]{:S(2)}) %collective-permute-start.7) | collective-permute-done | bytes 16416 | tf_op jit(solution)/shard_map/ppermute | solution.py:96
  22.0 1.1 %collective-permute-done.8.refs_5_ = bf16[16,256]{1,0:T(8,128)(2,1)S(1)} collective-permute-done((bf16[16,256]{1,0:T(8,128)(2,1)S(1)}, bf16[16,256]{1,0:T(8,128)(2,1)S(1)}, u32[]{:S(2)}, u32[]{:S(2)}) %collective-permute-start.8) | collective-permute-done | bytes 8224 | tf_op jit(solution)/shard_map/ppermute | solution.py:222
  23.1 0.6 %finish.1 = (bf16[16,256]{1,0:T(8,128)(2,1)}, bf16[16,256]{1,0:T(8,128)(2,1)}) custom-call(f32[16,256]{1,0:T(8,128)S(1)} %get-tuple-element.49.refs_0_, bf16[144,256]{1,0:T(8,128)(2,1)S(1)} %collective-permute-done.5.refs_6_.refs_1_, f32[16,256]{1,0:T(8,128)S(1)} %collective-permute-done.6.refs_2_, f32[16,256]{1,0:T(8,128)S(1)} %collective-permute-done.7.refs_3_, ...), custom_call_target="tpu_custom_call" | custom-call | tf_op jit(solution)/shard_map/finish/pallas_call | solution.py:249
  (1 shorter events, 0.0 us)
Async XLA Ops:
  0.6 6.2 %collective-permute-start = (bf16[16,256]{1,0:T(8,128)(2,1)}, bf16[16,256]{1,0:T(8,128)(2,1)S(1)}, u32[]{:S(2)}, u32[]{:S(2)}) collective-permute-start(bf16[16,256]{1,0:T(8,128)(2,1)} %feat_in.1), channel_id=1, source_target_pairs={{16,0},{0,16},{17,1},{1,17},{18,2},{2,18},{19,3},{3,19},{20,4},{4,... | collective-permute-start | bytes 24584 | tf_op jit(solution)/shard_map/ppermute | solution.py:222
  3.7 4.7 %collective-permute-start.1 = (bf16[16,256]{1,0:T(8,128)(2,1)}, bf16[16,256]{1,0:T(8,128)(2,1)S(1)}, u32[]{:S(2)}, u32[]{:S(2)}) collective-permute-start(bf16[16,256]{1,0:T(8,128)(2,1)} %cot_in.1), channel_id=1, source_target_pairs={{0,9},{1,8},{2,11},{3,10},{4,13},{5,12},{6,15},{7,14},{8,1},{9,0},... | collective-permute-start | bytes 24584 | tf_op jit(solution)/shard_map/ppermute | solution.py:96
  8.5 4.7 %collective-permute-start.2 = (bf16[96,256]{1,0:T(8,128)(2,1)S(1)}, bf16[96,256]{1,0:T(8,128)(2,1)S(1)}, u32[]{:S(2)}, u32[]{:S(2)}) collective-permute-start(bf16[96,256]{1,0:T(8,128)(2,1)S(1)} %get-tuple-element.46), channel_id=1, source_target_pairs={{0,4},{1,5},{2,6},{3,7},{4,0},{5,1},{6,2},{7,3},{8,12},{9,13},{10,... | collective-permute-start | bytes 147464 | tf_op jit(solution)/shard_map/ppermute | solution.py:96
  10.1 3.6 %collective-permute-start.3 = (bf16[96,256]{1,0:T(8,128)(2,1)S(1)}, bf16[96,256]{1,0:T(8,128)(2,1)S(1)}, u32[]{:S(2)}, u32[]{:S(2)}) collective-permute-start(bf16[96,256]{1,0:T(8,128)(2,1)S(1)} %get-tuple-element.47), channel_id=1, source_target_pairs={{0,5},{1,4},{2,7},{3,6},{4,1},{5,0},{6,3},{7,2},{8,13},{9,12},{10,... | collective-permute-start | bytes 147464 | tf_op jit(solution)/shard_map/ppermute | solution.py:96
  10.8 2.8 %collective-permute-start.4 = (bf16[96,256]{1,0:T(8,128)(2,1)S(1)}, bf16[96,256]{1,0:T(8,128)(2,1)S(1)}, u32[]{:S(2)}, u32[]{:S(2)}) collective-permute-start(bf16[96,256]{1,0:T(8,128)(2,1)S(1)} %get-tuple-element.48), channel_id=1, source_target_pairs={{0,1},{1,0},{2,3},{3,2},{4,5},{5,4},{6,7},{7,6},{8,9},{9,8},{10,11... | collective-permute-start | bytes 147464 | tf_op jit(solution)/shard_map/ppermute | solution.py:96
  13.7 4.4 %collective-permute-start.5 = (bf16[144,256]{1,0:T(8,128)(2,1)S(1)}, bf16[144,256]{1,0:T(8,128)(2,1)S(1)}, u32[]{:S(2)}, u32[]{:S(2)}) collective-permute-start(bf16[144,256]{1,0:T(8,128)(2,1)S(1)} %get-tuple-element.50), channel_id=1, source_target_pairs={{0,3},{1,2},{2,1},{3,0},{4,7},{5,6},{6,5},{7,4},{8,11},{9,10},{10,... | collective-permute-start | bytes 221192 | tf_op jit(solution)/shard_map/ppermute | solution.py:96
  15.5 5.7 %collective-permute-start.6 = (f32[16,256]{1,0:T(8,128)S(1)}, f32[16,256]{1,0:T(8,128)S(1)}, u32[]{:S(2)}, u32[]{:S(2)}) collective-permute-start(f32[16,256]{1,0:T(8,128)S(1)} %get-tuple-element.51), channel_id=1, source_target_pairs={{0,9},{1,8},{2,11},{3,10},{4,13},{5,12},{6,15},{7,14},{8,1},{9,0},... | collective-permute-start | bytes 49160 | tf_op jit(solution)/shard_map/ppermute | solution.py:96
  17.0 5.0 %collective-permute-start.7 = (f32[16,256]{1,0:T(8,128)S(1)}, f32[16,256]{1,0:T(8,128)S(1)}, u32[]{:S(2)}, u32[]{:S(2)}) collective-permute-start(f32[16,256]{1,0:T(8,128)S(1)} %get-tuple-element.52), channel_id=1, source_target_pairs={{0,11},{1,10},{2,9},{3,8},{4,15},{5,14},{6,13},{7,12},{8,3},{9,2},... | collective-permute-start | bytes 49160 | tf_op jit(solution)/shard_map/ppermute | solution.py:96
  19.4 3.7 %collective-permute-start.8 = (bf16[16,256]{1,0:T(8,128)(2,1)S(1)}, bf16[16,256]{1,0:T(8,128)(2,1)S(1)}, u32[]{:S(2)}, u32[]{:S(2)}) collective-permute-start(bf16[16,256]{1,0:T(8,128)(2,1)S(1)} %bitcast.4), channel_id=1, source_target_pairs={{16,0},{0,16},{17,1},{1,17},{18,2},{2,18},{19,3},{3,19},{20,4},{4,... | collective-permute-start | bytes 24584 | tf_op jit(solution)/shard_map/ppermute | solution.py:222

commit v4 on v3

--- a/solution.py
+++ b/solution.py
@@ -85,6 +85,10 @@
 def here():
     me = lax.axis_index("dst")
     return lax.div(me, NEAR * INNER), (me >> 1) & 1, ((me >> 2) & 1) * 2 + (me & 1)
+
+
+def layer_steps(n_far):
+    return [0, 1, *range(n_far * NEAR - 1, 1, -1)]
 
 
 def layer_partner(far, near, n_far, k):
@@ -170,14 +174,15 @@
             cots_out[part(f * INNER + whose, owned), :] = ref[f * owned : (f + 1) * owned, :]
     total[...] = sum((ref[:rows, :].astype(F32) for ref in parts), keep[...])
     for k, out in enumerate([own, *sends]):
-        layer = layer_partner(far, near, n_far, k)
+        layer = layer_partner(far, near, n_far, layer_steps(n_far)[k])
         out[:owned, :] = total[part(layer, owned), :].astype(out.dtype)
     sends[0][owned:, :] = cots_out[...]
 
 
 def slopes(_, half, w_node, w_out, slope_out, w_node_out, w_out_out):
     w_out_out[...] = w_out[...].T
-    w_node_out[...] = w_node[...].T
+    turned = w_node[...].T
+    w_node_out[...] = jnp.concatenate([turned, turned], axis=0)
     for c in chunks(half.shape[0]):
         t = jnp.tanh(half[c, :])
         slope_out[c, :] = 0.5 + 0.5 * (t + half[c, :] * (1.0 - t * t))
@@ -197,8 +202,8 @@
     for c in chunks(slope.shape[0]):
         d_message = dot(dst_hot[c, :], cots[...]).astype(BF16)
         d_pre[c, :] = (dot(d_message, w_out[...]) * slope[c, :]).astype(BF16)
-    high, low = halves(dot(src_hot[...], d_pre[...]))
-    total[...] = dot(high, w_node[...]) + dot(low, w_node[...])
+    parts = jnp.concatenate(halves(dot(src_hot[...], d_pre[...])), axis=1)
+    total[...] = dot(parts, w_node[...])
     me = lax.axis_index("src")
     keep_out[...] = total[part(me, owned), :]
     for k in range(1, n_src):
@@ -317,7 +322,7 @@
         slopes,
         "slopes",
         [keep, half, w_node, w_out],
-        [array(edges, hidden, dtype=F32)] + [array(*x.shape[::-1]) for x in (w_node, w_out)],
+        [array(edges, hidden, dtype=F32), array(2 * hidden, feat), array(*w_out.shape[::-1])],
     )
 
     beside = n_far * INNER
@@ -332,6 +337,7 @@
 
     def to_layer(i, k):
         far, near, me = place(i)
+        k = layer_steps(n_far)[k]
         far, near = partner_of(far, n_far, k // NEAR), partner_of(near, NEAR, k % NEAR)
         return block(far, near, me ^ 1)
 

time: 23.8 us -> 23.8 us (level)
    ppermute x7, waiting for transfers between devices: 1.89 us -> 1.37 us  [swap(): return [lax.ppermute(x, 'dst', pairs[k + 1]) for k, x in enumerate(sends)]]
    ppermute x2, waiting for transfers between devices: 1.08 us -> 1.59 us  [ahead(): return lax.ppermute(x, axis, [((i + k) % n, i) for i in range(n)])]
where the time goes in v4:
time: 23.8 us; the launch traced here: 23.7 us
  starting transfers between devices  12.1 us (51%)
  Pallas kernels  7.93 us (33%)
  waiting for transfers between devices  2.96 us (12%)
  between operations  0.7 us (3%)
    ppermute x7, starting transfers between devices, swap(): return [lax.ppermute(x, 'dst', pairs[k + 1]) for k, x in enumerate(sends)]  8.54 us
    pallas_call x8, Pallas kernels, call(): pl.pallas_call(kernel, name=name, in_specs=specs or [VMEM] * len(args), o...  7.93 us
    ppermute x2, starting transfers between devices, ahead(): return lax.ppermute(x, axis, [((i + k) % n, i) for i in range(n)])  3.56 us
    ppermute x2, waiting for transfers between devices, ahead(): return lax.ppermute(x, axis, [((i + k) % n, i) for i in range(n)])  1.59 us
    ppermute x7, waiting for transfers between devices, swap(): return [lax.ppermute(x, 'dst', pairs[k + 1]) for k, x in enumerate(sends)]  1.37 us
  transfers between devices with their start and end apart: 9, of which 4 were waited for; matrix products, arithmetic and copies ran while one was open for 0% of the time, Pallas kernels for 30%

profile of v4, /device:TPU:0, one launch (start us, length us, event | category | flops | bytes accessed | tf_op | source)
XLA Modules:
  0.0 23.7 jit_solution(3772730577889785864)
XLA Ops:
  0.6 3.0 %collective-permute-start = (bf16[16,256]{1,0:T(8,128)(2,1)}, bf16[16,256]{1,0:T(8,128)(2,1)S(1)}, u32[]{:S(2)}, u32[]{:S(2)}) collective-permute-start(bf16[16,256]{1,0:T(8,128)(2,1)} %feat_in.1), channel_id=1, source_target_pairs={{16,0},{0,16},{17,1},{1,17},{18,2},{2,18},{19,3},{3,19},{20,4},{4,... | collective-permute-start | bytes 24584 | tf_op jit(solution)/shard_map/ppermute | solution.py:227
  3.7 1.7 %collective-permute-start.1 = (bf16[16,256]{1,0:T(8,128)(2,1)}, bf16[16,256]{1,0:T(8,128)(2,1)S(1)}, u32[]{:S(2)}, u32[]{:S(2)}) collective-permute-start(bf16[16,256]{1,0:T(8,128)(2,1)} %cot_in.1), channel_id=1, source_target_pairs={{0,9},{1,8},{2,11},{3,10},{4,13},{5,12},{6,15},{7,14},{8,1},{9,0},... | collective-permute-start | bytes 24584 | tf_op jit(solution)/shard_map/ppermute | solution.py:100
  5.4 1.4 %prepare.1 = (bf16[1536,256]{1,0:T(8,128)(2,1)S(1)}, bf16[256,1536]{1,0:T(8,128)(2,1)S(1)}, bf16[1536,256]{1,0:T(8,128)(2,1)S(1)}, bf16[32,1536]{1,0:T(8,128)(2,...) custom-call(s32[12]{0:T(128)} %off_in.1, ...), custom_call_target="tpu_custom_call" | custom-call | tf_op jit(solution)/shard_map/prepare/pallas_call | solution.py:254
  6.8 0.0 collective-permute-done.refs_7_
  6.8 1.5 %forward.1 = (f32[1536,512]{1,0:T(8,128)S(1)}, f32[256,256]{1,0:T(8,128)S(1)}) custom-call(bf16[1536,256]{1,0:T(8,128)(2,1)S(1)} %get-tuple-element.33.refs_0_, bf16[256,1536]{1,0:T(8,128)(2,1)S(1)} %get-tuple-element.34.refs_1_, f32[1,512]{1,0:T(1,128)S(1)} %get-tuple-element.35.refs_2_, bf16[256,512]{1,0:T(8,128)(2,1)S(1)} %get-tuple-element.36.refs_3_.w_node, ...), custom_call_target="tpu_custom_call" | custom-call | tf_op jit(solution)/shard_map/forward/pallas_call | solution.py:254
  8.4 0.0 collective-permute-done.1.refs_2_
  8.4 0.1 pack.1
  8.5 1.6 %collective-permute-start.2 = (bf16[96,256]{1,0:T(8,128)(2,1)S(1)}, bf16[96,256]{1,0:T(8,128)(2,1)S(1)}, u32[]{:S(2)}, u32[]{:S(2)}) collective-permute-start(bf16[96,256]{1,0:T(8,128)(2,1)S(1)} %get-tuple-element.46), channel_id=1, source_target_pairs={{0,4},{1,5},{2,6},{3,7},{4,0},{5,1},{6,2},{7,3},{8,12},{9,13},{10,... | collective-permute-start | bytes 147464 | tf_op jit(solution)/shard_map/ppermute | solution.py:100
  10.1 0.7 %collective-permute-start.3 = (bf16[96,256]{1,0:T(8,128)(2,1)S(1)}, bf16[96,256]{1,0:T(8,128)(2,1)S(1)}, u32[]{:S(2)}, u32[]{:S(2)}) collective-permute-start(bf16[96,256]{1,0:T(8,128)(2,1)S(1)} %get-tuple-element.47), channel_id=1, source_target_pairs={{0,5},{1,4},{2,7},{3,6},{4,1},{5,0},{6,3},{7,2},{8,13},{9,12},{10,... | collective-permute-start | bytes 147464 | tf_op jit(solution)/shard_map/ppermute | solution.py:100
  10.8 0.0 collective-permute-start.4
  10.8 1.7 %slopes.1 = (f32[1536,512]{1,0:T(8,128)S(1)}, bf16[1024,256]{1,0:T(8,128)(2,1)S(1)}, bf16[256,512]{1,0:T(8,128)(2,1)S(1)}) custom-call(f32[64,256]{1,0:T(8,128)S(1)} %get-tuple-element.42._.refs_2_, f32[1536,512]{1,0:T(8,128)S(1)} %get-tuple-element.43.half, bf16[256,512]{1,0:T(8,128)(2,1)S(1)} %get-tuple-element.36.refs_3_.w_node, ...), custom_call_target="tpu_custom_call" | custom-call | tf_op jit(solution)/shard_map/slopes/pallas_call | solution.py:254
  12.5 0.6 %collective-permute-done.2.refs_3_ = bf16[96,256]{1,0:T(8,128)(2,1)S(1)} collective-permute-done((bf16[96,256]{1,0:T(8,128)(2,1)S(1)}, bf16[96,256]{1,0:T(8,128)(2,1)S(1)}, u32[]{:S(2)}, u32[]{:S(2)}) %collective-permute-start.2) | collective-permute-done | bytes 49184 | tf_op jit(solution)/shard_map/ppermute | solution.py:100
  13.1 0.5 %collective-permute-done.3.refs_4_ = bf16[96,256]{1,0:T(8,128)(2,1)S(1)} collective-permute-done((bf16[96,256]{1,0:T(8,128)(2,1)S(1)}, bf16[96,256]{1,0:T(8,128)(2,1)S(1)}, u32[]{:S(2)}, u32[]{:S(2)}) %collective-permute-start.3) | collective-permute-done | bytes 49184 | tf_op jit(solution)/shard_map/ppermute | solution.py:100
  13.7 0.0 collective-permute-done.4.refs_5_
  13.7 1.8 %collective-permute-start.5 = (bf16[144,256]{1,0:T(8,128)(2,1)S(1)}, bf16[144,256]{1,0:T(8,128)(2,1)S(1)}, u32[]{:S(2)}, u32[]{:S(2)}) collective-permute-start(bf16[144,256]{1,0:T(8,128)(2,1)S(1)} %get-tuple-element.50), channel_id=1, source_target_pairs={{0,3},{1,2},{2,1},{3,0},{4,7},{5,6},{6,5},{7,4},{8,11},{9,10},{10,... | collective-permute-start | bytes 221192 | tf_op jit(solution)/shard_map/ppermute | solution.py:100
  15.5 1.5 %collective-permute-start.6 = (f32[16,256]{1,0:T(8,128)S(1)}, f32[16,256]{1,0:T(8,128)S(1)}, u32[]{:S(2)}, u32[]{:S(2)}) collective-permute-start(f32[16,256]{1,0:T(8,128)S(1)} %get-tuple-element.51), channel_id=1, source_target_pairs={{0,11},{1,10},{2,9},{3,8},{4,15},{5,14},{6,13},{7,12},{8,3},{9,2},... | collective-permute-start | bytes 49160 | tf_op jit(solution)/shard_map/ppermute | solution.py:100
  17.0 1.1 %collective-permute-start.7 = (f32[16,256]{1,0:T(8,128)S(1)}, f32[16,256]{1,0:T(8,128)S(1)}, u32[]{:S(2)}, u32[]{:S(2)}) collective-permute-start(f32[16,256]{1,0:T(8,128)S(1)} %get-tuple-element.52), channel_id=1, source_target_pairs={{0,9},{1,8},{2,11},{3,10},{4,13},{5,12},{6,15},{7,14},{8,1},{9,0},... | collective-permute-start | bytes 49160 | tf_op jit(solution)/shard_map/ppermute | solution.py:100
  18.1 0.0 collective-permute-done.5.refs_6_.refs_1_
  18.1 1.3 %backward.1 = (bf16[1536,512]{1,0:T(8,128)(2,1)S(1)}, f32[16,256]{1,0:T(8,128)S(1)}, bf16[1,16,256]{2,1,0:T(8,128)(2,1)S(1)}) custom-call(f32[1536,512]{1,0:T(8,128)S(1)} %get-tuple-element.44.refs_0_, bf16[1536,256]{1,0:T(8,128)(2,1)S(1)} %get-tuple-element.53.refs_1_, bf16[32,1536]{1,0:T(8,128)(2,1)S(1)} %get-tuple-element.54.refs_2_, ...), custom_call_target="tpu_custom_call" | custom-call | tf_op jit(solution)/shard_map/backward/pallas_call | solution.py:254
  19.4 0.5 %collective-permute-start.8 = (bf16[16,256]{1,0:T(8,128)(2,1)S(1)}, bf16[16,256]{1,0:T(8,128)(2,1)S(1)}, u32[]{:S(2)}, u32[]{:S(2)}) collective-permute-start(bf16[16,256]{1,0:T(8,128)(2,1)S(1)} %bitcast.4), channel_id=1, source_target_pairs={{16,0},{0,16},{17,1},{1,17},{18,2},{2,18},{19,3},{3,19},{20,4},{4,... | collective-permute-start | bytes 24584 | tf_op jit(solution)/shard_map/ppermute | solution.py:227
  19.9 1.3 %attributes.1 = bf16[1536,128]{1,0:T(8,128)(2,1)} custom-call(bf16[1536,512]{1,0:T(8,128)(2,1)S(1)} %get-tuple-element.62.d_pre, bf16[128,512]{1,0:T(8,128)(2,1)S(1)} %get-tuple-element.37.refs_4_.w_edge), custom_call_target="tpu_custom_call" | custom-call | tf_op jit(solution)/shard_map/attributes/pallas_call | solution.py:254
  21.3 0.0 collective-permute-done.6.refs_2_
  21.3 0.2 collective-permute-done.7.refs_3_
  21.5 1.6 %collective-permute-done.8.refs_5_ = bf16[16,256]{1,0:T(8,128)(2,1)S(1)} collective-permute-done((bf16[16,256]{1,0:T(8,128)(2,1)S(1)}, bf16[16,256]{1,0:T(8,128)(2,1)S(1)}, u32[]{:S(2)}, u32[]{:S(2)}) %collective-permute-start.8) | collective-permute-done | bytes 8224 | tf_op jit(solution)/shard_map/ppermute | solution.py:227
  23.1 0.6 %finish.1 = (bf16[16,256]{1,0:T(8,128)(2,1)}, bf16[16,256]{1,0:T(8,128)(2,1)}) custom-call(f32[16,256]{1,0:T(8,128)S(1)} %get-tuple-element.49.refs_0_, bf16[144,256]{1,0:T(8,128)(2,1)S(1)} %collective-permute-done.5.refs_6_.refs_1_, f32[16,256]{1,0:T(8,128)S(1)} %collective-permute-done.6.refs_2_, f32[16,256]{1,0:T(8,128)S(1)} %collective-permute-done.7.refs_3_, ...), custom_call_target="tpu_custom_call" | custom-call | tf_op jit(solution)/shard_map/finish/pallas_call | solution.py:254
  (1 shorter events, 0.0 us)
Async XLA Ops:
  0.6 6.2 %collective-permute-start = (bf16[16,256]{1,0:T(8,128)(2,1)}, bf16[16,256]{1,0:T(8,128)(2,1)S(1)}, u32[]{:S(2)}, u32[]{:S(2)}) collective-permute-start(bf16[16,256]{1,0:T(8,128)(2,1)} %feat_in.1), channel_id=1, source_target_pairs={{16,0},{0,16},{17,1},{1,17},{18,2},{2,18},{19,3},{3,19},{20,4},{4,... | collective-permute-start | bytes 24584 | tf_op jit(solution)/shard_map/ppermute | solution.py:227
  3.7 4.7 %collective-permute-start.1 = (bf16[16,256]{1,0:T(8,128)(2,1)}, bf16[16,256]{1,0:T(8,128)(2,1)S(1)}, u32[]{:S(2)}, u32[]{:S(2)}) collective-permute-start(bf16[16,256]{1,0:T(8,128)(2,1)} %cot_in.1), channel_id=1, source_target_pairs={{0,9},{1,8},{2,11},{3,10},{4,13},{5,12},{6,15},{7,14},{8,1},{9,0},... | collective-permute-start | bytes 24584 | tf_op jit(solution)/shard_map/ppermute | solution.py:100
  8.5 4.7 %collective-permute-start.2 = (bf16[96,256]{1,0:T(8,128)(2,1)S(1)}, bf16[96,256]{1,0:T(8,128)(2,1)S(1)}, u32[]{:S(2)}, u32[]{:S(2)}) collective-permute-start(bf16[96,256]{1,0:T(8,128)(2,1)S(1)} %get-tuple-element.46), channel_id=1, source_target_pairs={{0,4},{1,5},{2,6},{3,7},{4,0},{5,1},{6,2},{7,3},{8,12},{9,13},{10,... | collective-permute-start | bytes 147464 | tf_op jit(solution)/shard_map/ppermute | solution.py:100
  10.1 3.6 %collective-permute-start.3 = (bf16[96,256]{1,0:T(8,128)(2,1)S(1)}, bf16[96,256]{1,0:T(8,128)(2,1)S(1)}, u32[]{:S(2)}, u32[]{:S(2)}) collective-permute-start(bf16[96,256]{1,0:T(8,128)(2,1)S(1)} %get-tuple-element.47), channel_id=1, source_target_pairs={{0,5},{1,4},{2,7},{3,6},{4,1},{5,0},{6,3},{7,2},{8,13},{9,12},{10,... | collective-permute-start | bytes 147464 | tf_op jit(solution)/shard_map/ppermute | solution.py:100
  10.8 2.8 %collective-permute-start.4 = (bf16[96,256]{1,0:T(8,128)(2,1)S(1)}, bf16[96,256]{1,0:T(8,128)(2,1)S(1)}, u32[]{:S(2)}, u32[]{:S(2)}) collective-permute-start(bf16[96,256]{1,0:T(8,128)(2,1)S(1)} %get-tuple-element.48), channel_id=1, source_target_pairs={{0,1},{1,0},{2,3},{3,2},{4,5},{5,4},{6,7},{7,6},{8,9},{9,8},{10,11... | collective-permute-start | bytes 147464 | tf_op jit(solution)/shard_map/ppermute | solution.py:100
  13.7 4.4 %collective-permute-start.5 = (bf16[144,256]{1,0:T(8,128)(2,1)S(1)}, bf16[144,256]{1,0:T(8,128)(2,1)S(1)}, u32[]{:S(2)}, u32[]{:S(2)}) collective-permute-start(bf16[144,256]{1,0:T(8,128)(2,1)S(1)} %get-tuple-element.50), channel_id=1, source_target_pairs={{0,3},{1,2},{2,1},{3,0},{4,7},{5,6},{6,5},{7,4},{8,11},{9,10},{10,... | collective-permute-start | bytes 221192 | tf_op jit(solution)/shard_map/ppermute | solution.py:100
  15.5 5.7 %collective-permute-start.6 = (f32[16,256]{1,0:T(8,128)S(1)}, f32[16,256]{1,0:T(8,128)S(1)}, u32[]{:S(2)}, u32[]{:S(2)}) collective-permute-start(f32[16,256]{1,0:T(8,128)S(1)} %get-tuple-element.51), channel_id=1, source_target_pairs={{0,11},{1,10},{2,9},{3,8},{4,15},{5,14},{6,13},{7,12},{8,3},{9,2},... | collective-permute-start | bytes 49160 | tf_op jit(solution)/shard_map/ppermute | solution.py:100
  17.0 4.5 %collective-permute-start.7 = (f32[16,256]{1,0:T(8,128)S(1)}, f32[16,256]{1,0:T(8,128)S(1)}, u32[]{:S(2)}, u32[]{:S(2)}) collective-permute-start(f32[16,256]{1,0:T(8,128)S(1)} %get-tuple-element.52), channel_id=1, source_target_pairs={{0,9},{1,8},{2,11},{3,10},{4,13},{5,12},{6,15},{7,14},{8,1},{9,0},... | collective-permute-start | bytes 49160 | tf_op jit(solution)/shard_map/ppermute | solution.py:100
  19.4 3.7 %collective-permute-start.8 = (bf16[16,256]{1,0:T(8,128)(2,1)S(1)}, bf16[16,256]{1,0:T(8,128)(2,1)S(1)}, u32[]{:S(2)}, u32[]{:S(2)}) collective-permute-start(bf16[16,256]{1,0:T(8,128)(2,1)S(1)} %bitcast.4), channel_id=1, source_target_pairs={{16,0},{0,16},{17,1},{1,17},{18,2},{2,18},{19,3},{3,19},{20,4},{4,... | collective-permute-start | bytes 24584 | tf_op jit(solution)/shard_map/ppermute | solution.py:227

commit v5 on v3

--- a/solution.py
+++ b/solution.py
@@ -87,6 +87,10 @@
     return lax.div(me, NEAR * INNER), (me >> 1) & 1, ((me >> 2) & 1) * 2 + (me & 1)
 
 
+def layer_steps(n_far):
+    return [0, 1, *range(n_far * NEAR - 1, 1, -1)]
+
+
 def layer_partner(far, near, n_far, k):
     return partner(far, n_far, k // NEAR) * NEAR + partner(near, NEAR, k % NEAR)
 
@@ -98,7 +102,7 @@
 
 def prepare(
     off_in, cnt_in, rel_in, sid_in, attr_in, cot_in, feat_in, bias_in, w_node_in, w_edge_in, w_out_in,
-    rows_out, dst_out, turned_out, src_out, cot_out, feat_out, bias_out, w_node_out, w_edge_out,
+    rows_out, dst_out, src_out, cot_out, feat_out, bias_out, w_node_out, w_edge_out,
     w_out_out, off, cnt, rel, sid, sems,
 ):
     width = attr_in.shape[1]
@@ -114,7 +118,6 @@
     fill = [jnp.zeros((spare, rel.shape[1]), F32)] if spare else []
     for at, to_dst, to_src in edge_hots(off, cnt, rel, sid, dst_out.shape[0], src_out.shape[0]):
         dst_out[:, at] = to_dst.astype(BF16)
-        turned_out[at, :] = to_dst.T.astype(BF16)
         src_out[:, at] = to_src.astype(BF16)
         rows_out[at, width:] = jnp.concatenate([to_src] * PARTS + fill, axis=0).T.astype(BF16)
     wait(copies[4:])
@@ -170,12 +173,14 @@
             cots_out[part(f * INNER + whose, owned), :] = ref[f * owned : (f + 1) * owned, :]
     total[...] = sum((ref[:rows, :].astype(F32) for ref in parts), keep[...])
     for k, out in enumerate([own, *sends]):
-        layer = layer_partner(far, near, n_far, k)
+        layer = layer_partner(far, near, n_far, layer_steps(n_far)[k])
         out[:owned, :] = total[part(layer, owned), :].astype(out.dtype)
     sends[0][owned:, :] = cots_out[...]
 
 
-def slopes(_, half, w_node, w_out, slope_out, w_node_out, w_out_out):
+def slopes(_, half, w_node, w_out, dst_hot, slope_out, w_node_out, w_out_out, turned_out):
+    for c in range(0, half.shape[0], 512):
+        turned_out[c : c + 512, :] = dst_hot[:, c : c + 512].astype(F32).T.astype(BF16)
     w_out_out[...] = w_out[...].T
     w_node_out[...] = w_node[...].T
     for c in chunks(half.shape[0]):
@@ -262,14 +267,13 @@
     depth = attr_width + PARTS * src_rows
     depth += -depth % 128
 
-    rows, dst_hot, turned, src_hot, cots, own, *params_near = call(
+    rows, dst_hot, src_hot, cots, own, *params_near = call(
         prepare,
         "prepare",
         [in_hbm(x) for x in (*ints, edge_attr, cotangent, node_feats, bias, w_node, w_edge, w_out)],
         [
             array(edges, depth),
             array(dst_rows, edges),
-            array(edges, dst_rows),
             array(src_rows, edges),
             rows_of(1),
             rows_of(1),
@@ -313,11 +317,12 @@
 
     parts = swap(sends, to_inner)
 
-    slope, w_node, w_out = call(
+    slope, w_node, w_out, turned = call(
         slopes,
         "slopes",
-        [keep, half, w_node, w_out],
-        [array(edges, hidden, dtype=F32)] + [array(*x.shape[::-1]) for x in (w_node, w_out)],
+        [keep, half, w_node, w_out, dst_hot],
+        [array(edges, hidden, dtype=F32)]
+        + [array(*x.shape[::-1]) for x in (w_node, w_out, dst_hot)],
     )
 
     beside = n_far * INNER
@@ -332,6 +337,7 @@
 
     def to_layer(i, k):
         far, near, me = place(i)
+        k = layer_steps(n_far)[k]
         far, near = partner_of(far, n_far, k // NEAR), partner_of(near, NEAR, k % NEAR)
         return block(far, near, me ^ 1)
 

time: 23.8 us -> 23.8 us (level)
    ppermute x7, waiting for transfers between devices: 1.89 us -> 1.17 us  [swap(): return [lax.ppermute(x, 'dst', pairs[k + 1]) for k, x in enumerate(sends)]]
    ppermute x2, waiting for transfers between devices: 1.08 us -> 1.59 us  [ahead(): return lax.ppermute(x, axis, [((i + k) % n, i) for i in range(n)])]
  transfers between devices with their start and end apart: 9 -> 9, of which waited for: 4 -> 4; matrix products, arithmetic and copies ran while one was open for 0% -> 0% of each run, Pallas kernels for 30% -> 31%
where the time goes in v5:
time: 23.8 us; the launch traced here: 23.7 us
  starting transfers between devices  12.1 us (51%)
  Pallas kernels  8.13 us (34%)
  waiting for transfers between devices  2.75 us (12%)
  between operations  0.7 us (3%)
    ppermute x7, starting transfers between devices, swap(): return [lax.ppermute(x, 'dst', pairs[k + 1]) for k, x in enumerate(sends)]  8.54 us
    pallas_call x8, Pallas kernels, call(): pl.pallas_call(kernel, name=name, in_specs=specs or [VMEM] * len(args), o...  8.13 us
    ppermute x2, starting transfers between devices, ahead(): return lax.ppermute(x, axis, [((i + k) % n, i) for i in range(n)])  3.56 us
    ppermute x2, waiting for transfers between devices, ahead(): return lax.ppermute(x, axis, [((i + k) % n, i) for i in range(n)])  1.59 us
    ppermute x7, waiting for transfers between devices, swap(): return [lax.ppermute(x, 'dst', pairs[k + 1]) for k, x in enumerate(sends)]  1.17 us
  transfers between devices with their start and end apart: 9, of which 4 were waited for; matrix products, arithmetic and copies ran while one was open for 0% of the time, Pallas kernels for 31%

profile of v5, /device:TPU:0, one launch (start us, length us, event | category | flops | bytes accessed | tf_op | source)
XLA Modules:
  0.0 23.7 jit_solution(13810032514932834726)
XLA Ops:
  0.6 3.0 %collective-permute-start = (bf16[16,256]{1,0:T(8,128)(2,1)}, bf16[16,256]{1,0:T(8,128)(2,1)S(1)}, u32[]{:S(2)}, u32[]{:S(2)}) collective-permute-start(bf16[16,256]{1,0:T(8,128)(2,1)} %feat_in.1), channel_id=1, source_target_pairs={{16,0},{0,16},{17,1},{1,17},{18,2},{2,18},{19,3},{3,19},{20,4},{4,... | collective-permute-start | bytes 24584 | tf_op jit(solution)/shard_map/ppermute | solution.py:227
  3.7 1.7 %collective-permute-start.1 = (bf16[16,256]{1,0:T(8,128)(2,1)}, bf16[16,256]{1,0:T(8,128)(2,1)S(1)}, u32[]{:S(2)}, u32[]{:S(2)}) collective-permute-start(bf16[16,256]{1,0:T(8,128)(2,1)} %cot_in.1), channel_id=1, source_target_pairs={{0,9},{1,8},{2,11},{3,10},{4,13},{5,12},{6,15},{7,14},{8,1},{9,0},... | collective-permute-start | bytes 24584 | tf_op jit(solution)/shard_map/ppermute | solution.py:100
  5.4 1.4 %prepare.1 = (bf16[1536,256]{1,0:T(8,128)(2,1)S(1)}, bf16[256,1536]{1,0:T(8,128)(2,1)S(1)}, bf16[32,1536]{1,0:T(8,128)(2,1)S(1)}, bf16[16,256]{1,0:T(8,128)(2,1)...) custom-call(s32[12]{0:T(128)} %off_in.1, ...), custom_call_target="tpu_custom_call" | custom-call | tf_op jit(solution)/shard_map/prepare/pallas_call | solution.py:254
  6.8 0.0 collective-permute-done.refs_7_
  6.8 1.5 %forward.1 = (f32[1536,512]{1,0:T(8,128)S(1)}, f32[256,256]{1,0:T(8,128)S(1)}) custom-call(bf16[1536,256]{1,0:T(8,128)(2,1)S(1)} %get-tuple-element.33.refs_0_, bf16[256,1536]{1,0:T(8,128)(2,1)S(1)} %get-tuple-element.34.refs_1_.dst_hot, f32[1,512]{1,0:T(1,128)S(1)} %get-tuple-element.35.refs_2_, bf16[256,512]{1,0:T(8,128)(2,1)S(1)} %get-tuple-element.36.refs_3_.w_node, ...), custom_call_target="tpu_custom_call" | custom-call | tf_op jit(solution)/shard_map/forward/pallas_call | solution.py:254
  8.4 0.0 collective-permute-done.1.refs_2_
  8.4 0.1 pack.1
  8.5 1.6 %collective-permute-start.2 = (bf16[96,256]{1,0:T(8,128)(2,1)S(1)}, bf16[96,256]{1,0:T(8,128)(2,1)S(1)}, u32[]{:S(2)}, u32[]{:S(2)}) collective-permute-start(bf16[96,256]{1,0:T(8,128)(2,1)S(1)} %get-tuple-element.46), channel_id=1, source_target_pairs={{0,4},{1,5},{2,6},{3,7},{4,0},{5,1},{6,2},{7,3},{8,12},{9,13},{10,... | collective-permute-start | bytes 147464 | tf_op jit(solution)/shard_map/ppermute | solution.py:100
  10.1 0.7 %collective-permute-start.3 = (bf16[96,256]{1,0:T(8,128)(2,1)S(1)}, bf16[96,256]{1,0:T(8,128)(2,1)S(1)}, u32[]{:S(2)}, u32[]{:S(2)}) collective-permute-start(bf16[96,256]{1,0:T(8,128)(2,1)S(1)} %get-tuple-element.47), channel_id=1, source_target_pairs={{0,5},{1,4},{2,7},{3,6},{4,1},{5,0},{6,3},{7,2},{8,13},{9,12},{10,... | collective-permute-start | bytes 147464 | tf_op jit(solution)/shard_map/ppermute | solution.py:100
  10.8 0.0 collective-permute-start.4
  10.8 1.9 %slopes.1 = (f32[1536,512]{1,0:T(8,128)S(1)}, bf16[512,256]{1,0:T(8,128)(2,1)S(1)}, bf16[256,512]{1,0:T(8,128)(2,1)S(1)}, bf16[1536,256]{1,0:T(8,128)(2,1)S(1)}) custom-call(f32[64,256]{1,0:T(8,128)S(1)} %get-tuple-element.42._.refs_2_, f32[1536,512]{1,0:T(8,128)S(1)} %get-tuple-element.43.half, bf16[256,512]{1,0:T(8,128)(2,1)S(1)} %get-tuple-element.36.refs_3_.w_node, ...), custom_call_target="tpu_custom_call" | custom-call | tf_op jit(solution)/shard_map/slopes/pallas_call | solution.py:254
  12.7 0.4 %collective-permute-done.2.refs_3_ = bf16[96,256]{1,0:T(8,128)(2,1)S(1)} collective-permute-done((bf16[96,256]{1,0:T(8,128)(2,1)S(1)}, bf16[96,256]{1,0:T(8,128)(2,1)S(1)}, u32[]{:S(2)}, u32[]{:S(2)}) %collective-permute-start.2) | collective-permute-done | bytes 49184 | tf_op jit(solution)/shard_map/ppermute | solution.py:100
  13.1 0.5 %collective-permute-done.3.refs_4_ = bf16[96,256]{1,0:T(8,128)(2,1)S(1)} collective-permute-done((bf16[96,256]{1,0:T(8,128)(2,1)S(1)}, bf16[96,256]{1,0:T(8,128)(2,1)S(1)}, u32[]{:S(2)}, u32[]{:S(2)}) %collective-permute-start.3) | collective-permute-done | bytes 49184 | tf_op jit(solution)/shard_map/ppermute | solution.py:100
  13.7 0.0 collective-permute-done.4.refs_5_
  13.7 1.8 %collective-permute-start.5 = (bf16[144,256]{1,0:T(8,128)(2,1)S(1)}, bf16[144,256]{1,0:T(8,128)(2,1)S(1)}, u32[]{:S(2)}, u32[]{:S(2)}) collective-permute-start(bf16[144,256]{1,0:T(8,128)(2,1)S(1)} %get-tuple-element.50), channel_id=1, source_target_pairs={{0,3},{1,2},{2,1},{3,0},{4,7},{5,6},{6,5},{7,4},{8,11},{9,10},{10,... | collective-permute-start | bytes 221192 | tf_op jit(solution)/shard_map/ppermute | solution.py:100
  15.5 1.5 %collective-permute-start.6 = (f32[16,256]{1,0:T(8,128)S(1)}, f32[16,256]{1,0:T(8,128)S(1)}, u32[]{:S(2)}, u32[]{:S(2)}) collective-permute-start(f32[16,256]{1,0:T(8,128)S(1)} %get-tuple-element.51), channel_id=1, source_target_pairs={{0,11},{1,10},{2,9},{3,8},{4,15},{5,14},{6,13},{7,12},{8,3},{9,2},... | collective-permute-start | bytes 49160 | tf_op jit(solution)/shard_map/ppermute | solution.py:100
  17.0 1.1 %collective-permute-start.7 = (f32[16,256]{1,0:T(8,128)S(1)}, f32[16,256]{1,0:T(8,128)S(1)}, u32[]{:S(2)}, u32[]{:S(2)}) collective-permute-start(f32[16,256]{1,0:T(8,128)S(1)} %get-tuple-element.52), channel_id=1, source_target_pairs={{0,9},{1,8},{2,11},{3,10},{4,13},{5,12},{6,15},{7,14},{8,1},{9,0},... | collective-permute-start | bytes 49160 | tf_op jit(solution)/shard_map/ppermute | solution.py:100
  18.1 0.0 collective-permute-done.5.refs_6_.refs_1_
  18.1 1.3 %backward.1 = (bf16[1536,512]{1,0:T(8,128)(2,1)S(1)}, f32[16,256]{1,0:T(8,128)S(1)}, bf16[1,16,256]{2,1,0:T(8,128)(2,1)S(1)}) custom-call(f32[1536,512]{1,0:T(8,128)S(1)} %get-tuple-element.44.refs_0_, bf16[1536,256]{1,0:T(8,128)(2,1)S(1)} %get-tuple-element.53.refs_1_, bf16[32,1536]{1,0:T(8,128)(2,1)S(1)} %get-tuple-element.54.refs_2_, ...), custom_call_target="tpu_custom_call" | custom-call | tf_op jit(solution)/shard_map/backward/pallas_call | solution.py:254
  19.4 0.5 %collective-permute-start.8 = (bf16[16,256]{1,0:T(8,128)(2,1)S(1)}, bf16[16,256]{1,0:T(8,128)(2,1)S(1)}, u32[]{:S(2)}, u32[]{:S(2)}) collective-permute-start(bf16[16,256]{1,0:T(8,128)(2,1)S(1)} %bitcast.4), channel_id=1, source_target_pairs={{16,0},{0,16},{17,1},{1,17},{18,2},{2,18},{19,3},{3,19},{20,4},{4,... | collective-permute-start | bytes 24584 | tf_op jit(solution)/shard_map/ppermute | solution.py:227
  19.9 1.3 %attributes.1 = bf16[1536,128]{1,0:T(8,128)(2,1)} custom-call(bf16[1536,512]{1,0:T(8,128)(2,1)S(1)} %get-tuple-element.62.d_pre, bf16[128,512]{1,0:T(8,128)(2,1)S(1)} %get-tuple-element.37.refs_4_.w_edge), custom_call_target="tpu_custom_call" | custom-call | tf_op jit(solution)/shard_map/attributes/pallas_call | solution.py:254
  21.2 0.0 collective-permute-done.6.refs_2_
  21.2 0.2 %collective-permute-done.7.refs_3_ = f32[16,256]{1,0:T(8,128)S(1)} collective-permute-done((f32[16,256]{1,0:T(8,128)S(1)}, f32[16,256]{1,0:T(8,128)S(1)}, u32[]{:S(2)}, u32[]{:S(2)}) %collective-permute-start.7) | collective-permute-done | bytes 16416 | tf_op jit(solution)/shard_map/ppermute | solution.py:100
  21.5 1.6 %collective-permute-done.8.refs_5_ = bf16[16,256]{1,0:T(8,128)(2,1)S(1)} collective-permute-done((bf16[16,256]{1,0:T(8,128)(2,1)S(1)}, bf16[16,256]{1,0:T(8,128)(2,1)S(1)}, u32[]{:S(2)}, u32[]{:S(2)}) %collective-permute-start.8) | collective-permute-done | bytes 8224 | tf_op jit(solution)/shard_map/ppermute | solution.py:227
  23.1 0.6 %finish.1 = (bf16[16,256]{1,0:T(8,128)(2,1)}, bf16[16,256]{1,0:T(8,128)(2,1)}) custom-call(f32[16,256]{1,0:T(8,128)S(1)} %get-tuple-element.49.refs_0_, bf16[144,256]{1,0:T(8,128)(2,1)S(1)} %collective-permute-done.5.refs_6_.refs_1_, f32[16,256]{1,0:T(8,128)S(1)} %collective-permute-done.6.refs_2_, f32[16,256]{1,0:T(8,128)S(1)} %collective-permute-done.7.refs_3_, ...), custom_call_target="tpu_custom_call" | custom-call | tf_op jit(solution)/shard_map/finish/pallas_call | solution.py:254
  (1 shorter events, 0.0 us)
Async XLA Ops:
  0.6 6.2 %collective-permute-start = (bf16[16,256]{1,0:T(8,128)(2,1)}, bf16[16,256]{1,0:T(8,128)(2,1)S(1)}, u32[]{:S(2)}, u32[]{:S(2)}) collective-permute-start(bf16[16,256]{1,0:T(8,128)(2,1)} %feat_in.1), channel_id=1, source_target_pairs={{16,0},{0,16},{17,1},{1,17},{18,2},{2,18},{19,3},{3,19},{20,4},{4,... | collective-permute-start | bytes 24584 | tf_op jit(solution)/shard_map/ppermute | solution.py:227
  3.7 4.7 %collective-permute-start.1 = (bf16[16,256]{1,0:T(8,128)(2,1)}, bf16[16,256]{1,0:T(8,128)(2,1)S(1)}, u32[]{:S(2)}, u32[]{:S(2)}) collective-permute-start(bf16[16,256]{1,0:T(8,128)(2,1)} %cot_in.1), channel_id=1, source_target_pairs={{0,9},{1,8},{2,11},{3,10},{4,13},{5,12},{6,15},{7,14},{8,1},{9,0},... | collective-permute-start | bytes 24584 | tf_op jit(solution)/shard_map/ppermute | solution.py:100
  8.5 4.7 %collective-permute-start.2 = (bf16[96,256]{1,0:T(8,128)(2,1)S(1)}, bf16[96,256]{1,0:T(8,128)(2,1)S(1)}, u32[]{:S(2)}, u32[]{:S(2)}) collective-permute-start(bf16[96,256]{1,0:T(8,128)(2,1)S(1)} %get-tuple-element.46), channel_id=1, source_target_pairs={{0,4},{1,5},{2,6},{3,7},{4,0},{5,1},{6,2},{7,3},{8,12},{9,13},{10,... | collective-permute-start | bytes 147464 | tf_op jit(solution)/shard_map/ppermute | solution.py:100
  10.1 3.6 %collective-permute-start.3 = (bf16[96,256]{1,0:T(8,128)(2,1)S(1)}, bf16[96,256]{1,0:T(8,128)(2,1)S(1)}, u32[]{:S(2)}, u32[]{:S(2)}) collective-permute-start(bf16[96,256]{1,0:T(8,128)(2,1)S(1)} %get-tuple-element.47), channel_id=1, source_target_pairs={{0,5},{1,4},{2,7},{3,6},{4,1},{5,0},{6,3},{7,2},{8,13},{9,12},{10,... | collective-permute-start | bytes 147464 | tf_op jit(solution)/shard_map/ppermute | solution.py:100
  10.8 2.8 %collective-permute-start.4 = (bf16[96,256]{1,0:T(8,128)(2,1)S(1)}, bf16[96,256]{1,0:T(8,128)(2,1)S(1)}, u32[]{:S(2)}, u32[]{:S(2)}) collective-permute-start(bf16[96,256]{1,0:T(8,128)(2,1)S(1)} %get-tuple-element.48), channel_id=1, source_target_pairs={{0,1},{1,0},{2,3},{3,2},{4,5},{5,4},{6,7},{7,6},{8,9},{9,8},{10,11... | collective-permute-start | bytes 147464 | tf_op jit(solution)/shard_map/ppermute | solution.py:100
  13.7 4.4 %collective-permute-start.5 = (bf16[144,256]{1,0:T(8,128)(2,1)S(1)}, bf16[144,256]{1,0:T(8,128)(2,1)S(1)}, u32[]{:S(2)}, u32[]{:S(2)}) collective-permute-start(bf16[144,256]{1,0:T(8,128)(2,1)S(1)} %get-tuple-element.50), channel_id=1, source_target_pairs={{0,3},{1,2},{2,1},{3,0},{4,7},{5,6},{6,5},{7,4},{8,11},{9,10},{10,... | collective-permute-start | bytes 221192 | tf_op jit(solution)/shard_map/ppermute | solution.py:100
  15.5 5.7 %collective-permute-start.6 = (f32[16,256]{1,0:T(8,128)S(1)}, f32[16,256]{1,0:T(8,128)S(1)}, u32[]{:S(2)}, u32[]{:S(2)}) collective-permute-start(f32[16,256]{1,0:T(8,128)S(1)} %get-tuple-element.51), channel_id=1, source_target_pairs={{0,11},{1,10},{2,9},{3,8},{4,15},{5,14},{6,13},{7,12},{8,3},{9,2},... | collective-permute-start | bytes 49160 | tf_op jit(solution)/shard_map/ppermute | solution.py:100
  17.0 4.5 %collective-permute-start.7 = (f32[16,256]{1,0:T(8,128)S(1)}, f32[16,256]{1,0:T(8,128)S(1)}, u32[]{:S(2)}, u32[]{:S(2)}) collective-permute-start(f32[16,256]{1,0:T(8,128)S(1)} %get-tuple-element.52), channel_id=1, source_target_pairs={{0,9},{1,8},{2,11},{3,10},{4,13},{5,12},{6,15},{7,14},{8,1},{9,0},... | collective-permute-start | bytes 49160 | tf_op jit(solution)/shard_map/ppermute | solution.py:100
  19.4 3.7 %collective-permute-start.8 = (bf16[16,256]{1,0:T(8,128)(2,1)S(1)}, bf16[16,256]{1,0:T(8,128)(2,1)S(1)}, u32[]{:S(2)}, u32[]{:S(2)}) collective-permute-start(bf16[16,256]{1,0:T(8,128)(2,1)S(1)} %bitcast.4), channel_id=1, source_target_pairs={{16,0},{0,16},{17,1},{1,17},{18,2},{2,18},{19,3},{3,19},{20,4},{4,... | collective-permute-start | bytes 24584 | tf_op jit(solution)/shard_map/ppermute | solution.py:227
